TPU v7x, 256 devices: a whole 4x4x8 slice. The times are simulated.
256 devices in a mesh: node: 4 (over x), rail: 64 (over z, y, core).
Axes of the slice: x: 4, y: 4, z: 8, core: 2. Of those that a mesh axis runs over, the one named last changes fastest.
Arguments:
- queries: bfloat16 [16384, 4096], P(('rail', 'node')), may hold values from -6 to 6, as said below
- keys: bfloat16 [16384, 512], P(('rail', 'node')), may hold values from -6 to 6, as said below
- values: bfloat16 [16384, 512], P(('rail', 'node')), may hold values from -6 to 6
- output_cotangent: bfloat16 [16384, 4096], P(('rail', 'node')), may hold values from -6 to 6
- doc_lengths: int32 [16], replicated, may hold values from 1 to 2048, 16384 in all
- span_slot: int32 [128], replicated, may hold values from 0 to 127, each once
Outputs:
- d_queries: bfloat16 [16384, 4096], P(('rail', 'node'))
- keys_gradient: bfloat16 [16384, 512], P(('rail', 'node'))
- values_gradient: bfloat16 [16384, 512], P(('rail', 'node'))
Inputs may be any that keep to these rules, and one draw needn't show every extreme that they name: queries lie within this range in every draw. keys lie within this range in every draw. `span_slot`: a permutation of the slots.
All inputs are finite; a program needn't handle non-finite values.
Results may differ from a plain program's by a relative error of at most 0.0075.
Values may be sent and summed in bfloat16 or wider, within the bound.
A program may use at most 128 MiB of HBM per device.

v0:
```python
import math

import jax
import jax.numpy as jnp
from jax import lax
from jax.sharding import PartitionSpec as P

HEAD_SIZE = 128
QUERY_GROUP = 8


def slot_spans(span_slot):
    slot_count = span_slot.shape[0]
    numbers = jnp.arange(slot_count, dtype=jnp.int32)
    return jnp.sum(jnp.where(span_slot[:, None] == numbers[None, :], numbers[:, None], 0), axis=0)


def doc_number(places, doc_ends):
    return jnp.sum((places[:, None] >= doc_ends[None, :]).astype(jnp.int32), axis=1)


def per_device(queries, keys, values, output_cotangent, doc_lengths, span_slot):
    softmax_scale = 1.0 / math.sqrt(HEAD_SIZE)
    q_mid, o_mid, k_mid, v_mid = (
        lax.all_to_all(queries, "node", split_axis=1, concat_axis=0, tiled=True),
        lax.all_to_all(output_cotangent, "node", split_axis=1, concat_axis=0, tiled=True),
        lax.all_to_all(keys, "node", split_axis=1, concat_axis=0, tiled=True),
        lax.all_to_all(values, "node", split_axis=1, concat_axis=0, tiled=True),
    )
    rows_mid = q_mid.shape[0]
    span_rows = rows_mid // 2
    slot_count = span_slot.shape[0]
    seq_rows = slot_count * span_rows
    doc_reach = seq_rows // 8
    win_rows = doc_reach + span_rows
    heads_kv = k_mid.shape[1] // HEAD_SIZE
    span_of_slot = slot_spans(span_slot)
    doc_ends = jnp.cumsum(doc_lengths)
    rail_place = lax.axis_index("rail")
    offsets = jnp.arange(win_rows, dtype=jnp.int32)
    within = jnp.arange(span_rows, dtype=jnp.int32)
    window_rows = []
    allowed_all = []
    for half_id in range(2):
        start_place = span_of_slot[rail_place * 2 + half_id] * span_rows
        query_places = start_place + within
        win_places = start_place - doc_reach + offsets
        in_range = win_places >= 0
        clamped = jnp.maximum(win_places, 0)
        window_rows.append(
            jnp.take(span_slot, clamped // span_rows) * span_rows + clamped % span_rows
        )
        win_docs = jnp.where(in_range, doc_number(clamped, doc_ends), -1)
        query_docs = doc_number(query_places, doc_ends)
        allowed_all.append(
            (win_docs[None, :] == query_docs[:, None])
            & (win_places[None, :] <= query_places[:, None])
        )
    rows_both = jnp.stack(window_rows)
    k_all, v_all = (
        lax.all_gather(k_mid, "rail", axis=0, tiled=True),
        lax.all_gather(v_mid, "rail", axis=0, tiled=True),
    )
    k_win = jnp.take(k_all, rows_both, axis=0)
    v_win = jnp.take(v_all, rows_both, axis=0)
    part_keys = jnp.zeros((seq_rows, k_mid.shape[1]), jnp.float32)
    part_values = jnp.zeros((seq_rows, k_mid.shape[1]), jnp.float32)
    query_grads = []
    for half_id in range(2):
        lower = half_id * span_rows
        query_blk = q_mid[lower : lower + span_rows].reshape(
            span_rows, heads_kv, QUERY_GROUP, HEAD_SIZE
        )
        grad_blk = o_mid[lower : lower + span_rows].reshape(
            span_rows, heads_kv, QUERY_GROUP, HEAD_SIZE
        )
        key_blk = k_win[half_id].reshape(win_rows, heads_kv, HEAD_SIZE)
        value_blk = v_win[half_id].reshape(win_rows, heads_kv, HEAD_SIZE)
        scores = (
            jnp.einsum("qhgd,khd->hgqk", query_blk, key_blk, preferred_element_type=jnp.float32)
            * softmax_scale
        )
        scores = jnp.where(allowed_all[half_id][None, None], scores, -jnp.inf)
        row_max = jnp.max(scores, axis=-1, keepdims=True)
        log_total = row_max + jnp.log(jnp.sum(jnp.exp(scores - row_max), axis=-1, keepdims=True))
        probs = jnp.exp(scores - log_total)
        d_probs = jnp.einsum(
            "qhgd,khd->hgqk", grad_blk, value_blk, preferred_element_type=jnp.float32
        )
        row_dots = jnp.sum(probs * d_probs, axis=-1, keepdims=True)
        d_scores_b = (probs * (d_probs - row_dots)).astype(jnp.bfloat16)
        probs_b = probs.astype(jnp.bfloat16)
        query_grad = (
            jnp.einsum("hgqk,khd->qhgd", d_scores_b, key_blk, preferred_element_type=jnp.float32)
            * softmax_scale
        )
        query_grads.append(query_grad.astype(jnp.bfloat16).reshape(span_rows, -1))
        key_part = (
            jnp.einsum("hgqk,qhgd->khd", d_scores_b, query_blk, preferred_element_type=jnp.float32)
            * softmax_scale
        )
        value_part = jnp.einsum(
            "hgqk,qhgd->khd", probs_b, grad_blk, preferred_element_type=jnp.float32
        )
        part_keys = part_keys.at[rows_both[half_id]].add(key_part.reshape(win_rows, -1))
        part_values = part_values.at[rows_both[half_id]].add(value_part.reshape(win_rows, -1))
    dq_mid = jnp.concatenate(query_grads, axis=0)
    key_sums, value_sums = (
        lax.psum_scatter(part_keys, "rail", scatter_dimension=0, tiled=True),
        lax.psum_scatter(part_values, "rail", scatter_dimension=0, tiled=True),
    )
    key_mid = key_sums.astype(jnp.bfloat16)
    value_mid = value_sums.astype(jnp.bfloat16)
    dq_back, dk_back, dv_back = (
        lax.all_to_all(dq_mid, "node", split_axis=0, concat_axis=1, tiled=True),
        lax.all_to_all(key_mid, "node", split_axis=0, concat_axis=1, tiled=True),
        lax.all_to_all(value_mid, "node", split_axis=0, concat_axis=1, tiled=True),
    )
    return (dq_back, dk_back, dv_back)


def solution(mesh):
    in_specs = (
        P(("rail", "node"), None),
        P(("rail", "node"), None),
        P(("rail", "node"), None),
        P(("rail", "node"), None),
        P(),
        P(),
    )
    out_specs = (P(("rail", "node"), None), P(("rail", "node"), None), P(("rail", "node"), None))
    return jax.shard_map(
        per_device, mesh=mesh, in_specs=in_specs, out_specs=out_specs, check_vma=False
    )
```

profile of v0, /device:TPU:2, one launch (start us, length us, event | category | flops | bytes accessed | tf_op | source)
XLA Modules:
  0.0 602.5 jit_solution(14082747623537890760)
XLA Ops:
  8.0 9.5 %all_to_all.127 = bf16[64,4,128]{2,0,1:T(8,128)(2,1)} all-to-all(bf16[64,4,128]{2,0,1:T(8,128)(2,1)S(1)} %copy_bitcast_fusion.5), channel_id=1, replica_groups=mesh['node'=4,'rail'=64] {'node'}, dimensions={1} | all-to-all | bytes 131072 | tf_op jit(solution)/shard_map/all_to_all | solution.py:27
  18.4 8.7 %all_to_all.128 = bf16[64,4,128]{2,0,1:T(8,128)(2,1)} all-to-all(bf16[64,4,128]{2,0,1:T(8,128)(2,1)S(1)} %copy_bitcast_fusion.4), channel_id=1, replica_groups=mesh['node'=4,'rail'=64] {'node'}, dimensions={1} | all-to-all | bytes 131072 | tf_op jit(solution)/shard_map/all_to_all | solution.py:28
  29.0 4.9 all-to-all-start.1
  36.0 12.6 %gather_fusion.1 = s32[2176]{0:T(1024)S(1)} fusion(s32[128]{0:T(128)S(1)} %copy-done.2, s32[3072]{0:T(1024)S(1)} %pad_clamp_fusion.1), kind=kCustom, calls=%fused_computation.2.clone | custom fusion | bytes 26112 | tf_op jit(solution)/shard_map/jit(_take)/gather | solution.py:51
  49.3 12.6 %gather_fusion = s32[2176]{0:T(1024)S(1)} fusion(s32[128]{0:T(128)S(1)} %copy-done.2, s32[3072]{0:T(1024)S(1)} %pad_clamp_fusion.2), kind=kCustom, calls=%fused_computation.clone | custom fusion | bytes 26112 | tf_op jit(solution)/shard_map/jit(_take)/gather | solution.py:51
  67.8 4.8 all-to-all-start.3
  73.4 5.7 all-to-all-done.3
  81.5 16.6 %all-gather.3.cloned.1.call-done = bf16[16384,128]{1,0:T(8,128)(2,1)} async-done(((bf16[256,128]{1,0:T(8,128)(2,1)}), bf16[16384,128]{1,0:T(8,128)(2,1)}) %all-gather.3.cloned.1.call-update) | async-done | bytes 4194320 | tf_op jit(solution)/shard_map/all_gather | solution.py:61
  98.2 10.0 %gather_fusion.2 = bf16[4352,128]{1,0:T(8,128)(2,1)S(1)} fusion(bf16[16384,128]{1,0:T(8,128)(2,1)} %all-gather.3.cloned.1.call-done, s32[5120]{0:T(1024)S(1)} %pad_clamp_fusion), kind=kCustom, calls=%fused_computation.1.clone | custom fusion | bytes 2245632 | tf_op jit(solution)/shard_map/jit(_take)/gather | solution.py:64
  108.2 69.1 %all-gather.5.cloned.1.call-done = bf16[16384,128]{1,0:T(8,128)(2,1)} async-done(((bf16[256,128]{1,0:T(8,128)(2,1)}), bf16[16384,128]{1,0:T(8,128)(2,1)}) %all-gather.5.cloned.1.call-update) | async-done | bytes 4194320 | tf_op jit(solution)/shard_map/all_gather | solution.py:62
  177.2 11.5 %gather_fusion.3 = bf16[4352,128]{1,0:T(8,128)(2,1)} fusion(bf16[16384,128]{1,0:T(8,128)(2,1)} %all-gather.5.cloned.1.call-done, s32[5120]{0:T(1024)S(1)} %pad_clamp_fusion), kind=kCustom, calls=%fused_computation.3.clone | custom fusion | bytes 2245632 | tf_op jit(solution)/shard_map/jit(_take)/gather | solution.py:65
  205.7 10.0 %fusion.14 = bf16[8,128,2176]{1,2,0:T(8,128)(2,1)} fusion(f32[2176,128,8]{1,0,2:T(8,128)} %get-tuple-element.30, f32[1,8,128,2176]{2,3,1,0:T(8,128)} %copy-done.4, f32[8,128]{1,0:T(8,128)S(1)} %get-tuple-element.29, f32[8,128]{1,0:T(8,128)S(1)} %log_add_fusion.1), kind=kLoop, calls=%fused_computation.30 | loop fusion | flops 8912896 | bytes 22290432 | tf_op jit(solution)/shard_map/reshape.33
  220.3 6.6 %fusion = (f32[8,128]{1,0:T(8,128)S(1)}, f32[2176,128,8]{1,0,2:T(8,128)}) fusion(f32[1,8,128,2176]{2,3,1,0:T(8,128)} %copy-done.3, f32[8,128]{1,0:T(8,128)S(1)} %log_add_fusion, bf16[128,8,128]{2,1,0:T(8,128)(2,1)S(1)} %bitcast.167, bf16[2,2176,128]{2,1,0:T(8,128)(2,1)S(1)} %get-tuple-element.20), kind=kOutput, calls=%fused_computation.12 | convolution fusion | flops 577108992 | bytes 18653184 | tf_op jit(solution)/shard_map/qhgd,khd->hgqk/dot_general | solution.py:87
  226.9 9.9 %fusion.15 = bf16[8,128,2176]{1,2,0:T(8,128)(2,1)} fusion(f32[2176,128,8]{1,0,2:T(8,128)} %get-tuple-element.26, f32[1,8,128,2176]{2,3,1,0:T(8,128)} %copy-done.3, f32[8,128]{1,0:T(8,128)S(1)} %get-tuple-element.25, f32[8,128]{1,0:T(8,128)S(1)} %log_add_fusion), kind=kLoop, calls=%fused_computation.31 | loop fusion | flops 8912896 | bytes 22290432 | tf_op jit(solution)/shard_map/reshape.50
  240.4 18.4 %scatter_custom_fusion = f32[16384,128]{1,0:T(8,128)} fusion(s32[2176]{0:T(1024)S(1)} %get-tuple-element.11, f32[2176,128]{1,0:T(8,128)} %fusion.29, f32[]{:T(128)} %constant.98.clone.1), kind=kCustom, calls=%fused_computation.36 | custom fusion | flops 278528 | bytes 8389120 | tf_op jit(solution)/shard_map/scatter-add | solution.py:105
  258.8 19.6 %scatter_fusion = f32[16384,128]{1,0:T(8,128)} fusion(f32[16384,128]{1,0:T(8,128)} %scatter_custom_fusion, s32[2176]{0:T(1024)S(1)} %get-tuple-element.9, f32[2176,128]{1,0:T(8,128)S(1)} %fusion.28), kind=kCustom, calls=%fused_computation.5 | custom fusion | flops 278528 | bytes 3351040 | tf_op jit(solution)/shard_map/scatter-add | solution.py:105
  278.5 4.9 fusion.22
  283.4 18.3 %scatter_custom_fusion.2 = f32[16384,128]{1,0:T(8,128)} fusion(s32[2176]{0:T(1024)S(1)} %get-tuple-element.11, f32[2176,128]{1,0:T(8,128)S(1)} %fusion.22, f32[]{:T(128)} %constant.98.clone.1), kind=kCustom, calls=%fused_computation.34 | custom fusion | flops 278528 | bytes 8388612 | tf_op jit(solution)/shard_map/scatter-add | solution.py:106
  301.7 5.1 fusion.25
  306.8 19.8 %scatter_fusion.1 = f32[16384,128]{1,0:T(8,128)} fusion(f32[16384,128]{1,0:T(8,128)} %scatter_custom_fusion.2, s32[2176]{0:T(1024)S(1)} %get-tuple-element.9, f32[2176,128]{1,0:T(8,128)S(1)} %fusion.25), kind=kCustom, calls=%fused_computation.7 | custom fusion | flops 278528 | bytes 3351040 | tf_op jit(solution)/shard_map/scatter-add | solution.py:106
  339.0 91.2 %reduce-scatter.3.cloned.1.call-done = f32[256,128]{1,0:T(8,128)} async-done(((f32[16384,128]{1,0:T(8,128)}), f32[256,128]{1,0:T(8,128)}) %reduce-scatter.3.cloned.1.call-update) | async-done | bytes 131088 | tf_op jit(solution)/shard_map/reduce_scatter | solution.py:109
  431.8 4.9 all-to-all-start.5
  437.5 147.4 %reduce-scatter.5.cloned.1.call-done = f32[256,128]{1,0:T(8,128)} async-done(((f32[16384,128]{1,0:T(8,128)}), f32[256,128]{1,0:T(8,128)}) %reduce-scatter.5.cloned.1.call-update) | async-done | bytes 131088 | tf_op jit(solution)/shard_map/reduce_scatter | solution.py:110
  586.4 4.8 all-to-all-start.6
  (95 shorter events, 60.2 us)
Async XLA Ops:
  7.2 0.8 copy-start
  7.2 28.8 %copy-start.2 = (s32[128]{0:T(128)S(1)}, s32[128]{0:T(128)}, u32[]{:S(2)}) copy-start(s32[128]{0:T(128)} %param.15) | copy-start | bytes 1540
  7.2 91.0 %all-gather.3.cloned.1.call-start = ((), (), s32[]{:S(2)}) async-start(), calls=%async_computation.9 | async-start | bytes 4259840 | tf_op jit(solution)/shard_map/all_gather | solution.py:61
  17.5 159.7 %all-gather.5.cloned.1.call-start = ((), (), s32[]{:S(2)}) async-start(), calls=%async_computation.10 | async-start | bytes 4259840 | tf_op jit(solution)/shard_map/all_gather | solution.py:62
  29.0 38.7 %all-to-all-start.1 = ((bf16[64,4,1024]{2,0,1:T(8,128)(2,1)}), bf16[64,4,1024]{2,0,1:T(8,128)(2,1)S(1)}, u32[]{:S(2)}, u32[]{:S(2)}) async-start(bf16[64,4,1024]{2,0,1:T(8,128)(2,1)} %bitcast.164), calls=%async_computation.1 | async-start | bytes 1048576 | tf_op jit(solution)/shard_map/all_to_all | solution.py:25
  49.3 12.7 %copy-start.13 = (s32[16]{0:T(128)S(1)}, s32[16]{0:T(128)}, u32[]{:S(2)}) copy-start(s32[16]{0:T(128)} %param.14) | copy-start | bytes 196
  49.3 12.9 %copy-start.10 = (bf16[64,4096]{1,0:T(8,128)(2,1)S(1)}, bf16[64,4096]{1,0:T(8,128)(2,1)}, u32[]{:S(2)}) copy-start(bf16[64,4096]{1,0:T(8,128)(2,1)} %param.13) | copy-start | bytes 1572868
  67.8 11.4 %all-to-all-start.3 = ((bf16[64,4,1024]{2,0,1:T(8,128)(2,1)}), bf16[64,4,1024]{2,0,1:T(8,128)(2,1)S(1)}, u32[]{:S(2)}, u32[]{:S(2)}) async-start(bf16[64,4,1024]{2,0,1:T(8,128)(2,1)} %bitcast.163), calls=%async_computation.3 | async-start | bytes 1048576 | tf_op jit(solution)/shard_map/all_to_all | solution.py:26
  72.6 357.7 %reduce-scatter.3.cloned.1.call-start = ((), (), s32[]{:S(2)}) async-start(), calls=%async_computation.11 | async-start | bytes 8519680 | tf_op jit(solution)/shard_map/reduce_scatter | solution.py:109
  188.7 2.9 copy-start.7
  188.7 2.9 copy-start.12
  193.0 3.4 copy-start.3
  193.0 3.4 copy-start.9
  193.0 3.4 copy-start.11
  197.7 3.5 copy-start.4
  197.7 3.5 copy-start.6
  215.7 4.6 copy-start.5
  226.9 9.9 %copy-start.8 = (bf16[16,8,8,128]{3,2,1,0:T(8,128)(2,1)S(1)}, bf16[16,8,8,128]{3,2,1,0:T(8,128)(2,1)}, u32[]{:S(2)}) copy-start(bf16[16,8,8,128]{3,2,1,0:T(8,128)(2,1)} %copy.95) | copy-start | bytes 786436
  278.4 306.4 %reduce-scatter.5.cloned.1.call-start = ((), (), s32[]{:S(2)}) async-start(), calls=%async_computation.12 | async-start | bytes 8519680 | tf_op jit(solution)/shard_map/reduce_scatter | solution.py:110
  330.0 266.0 %copy-start.1 = (bf16[64,512]{1,0:T(8,128)(2,1)S(1)}, bf16[64,512]{1,0:T(8,128)(2,1)}, u32[]{:S(2)}) copy-start(bf16[64,512]{1,0:T(8,128)(2,1)} %param.11) | copy-start | bytes 196612
  334.2 97.6 %all-to-all-start.4 = ((bf16[4,64,1024]{2,1,0:T(8,128)(2,1)}), bf16[4,64,1024]{2,1,0:T(8,128)(2,1)S(1)}, u32[]{:S(2)}, u32[]{:S(2)}) async-start(bf16[4,64,1024]{2,1,0:T(8,128)(2,1)} %bitcast.39), calls=%async_computation.4 | async-start | bytes 1048576 | tf_op jit(solution)/shard_map/all_to_all | solution.py:115
  431.8 154.6 %all-to-all-start.5 = ((bf16[4,64,128]{2,1,0:T(8,128)(2,1)}), bf16[4,64,128]{2,1,0:T(8,128)(2,1)S(1)}, u32[]{:S(2)}, u32[]{:S(2)}) async-start(bf16[4,64,128]{2,1,0:T(8,128)(2,1)} %bitcast.43), calls=%async_computation.6 | async-start | bytes 131072 | tf_op jit(solution)/shard_map/all_to_all | solution.py:116
  586.4 9.0 %all-to-all-start.6 = ((bf16[4,64,128]{2,1,0:T(8,128)(2,1)}), bf16[4,64,128]{2,1,0:T(8,128)(2,1)S(1)}, u32[]{:S(2)}, u32[]{:S(2)}) async-start(bf16[4,64,128]{2,1,0:T(8,128)(2,1)} %bitcast.49), calls=%async_computation.8 | async-start | bytes 131072 | tf_op jit(solution)/shard_map/all_to_all | solution.py:117
Sparse Core Ops, SparseCore 0:
  17.7 80.4 all-gather.2
  100.9 76.2 all-gather.4
  278.5 151.6 reduce-scatter.2
  434.9 149.9 reduce-scatter.4
where the time goes:
time: 604 us; the launch traced here: 603 us
  waiting for transfers between devices  334 us (55%)
  other arithmetic  111 us (18%)
  local copies, waits for them, and re-layouts  61.9 us (10%)
  matrix products  38.4 us (6%)
  starting transfers between devices  24.3 us (4%)
  blocking collectives  18.2 us (3%)
  between operations  15.4 us (3%)
    reduce_scatter x1, waiting for transfers between devices, per_device(): lax.psum_scatter(part_values, 'rail', scatter_dimension=0, tiled=True)  147 us
    reduce_scatter x1, waiting for transfers between devices, per_device(): lax.psum_scatter(part_keys, 'rail', scatter_dimension=0, tiled=True)  91.2 us
    all_gather x1, waiting for transfers between devices, per_device(): lax.all_gather(v_mid, 'rail', axis=0, tiled=True)  69.1 us
    scatter-add x2, other arithmetic, per_device(): part_values.at[rows_both[half_id]].add(value_part.reshape(win_rows, -1))  38.1 us
    scatter-add x2, other arithmetic, per_device(): part_keys.at[rows_both[half_id]].add(key_part.reshape(win_rows, -1))  38 us
    gather x2, local copies, waits for them, and re-layouts, per_device(): jnp.take(span_slot, clamped // span_rows) * span_rows + clamped % span_rows  25.2 us
    another operation x4, other arithmetic  20.1 us
    all_gather x1, waiting for transfers between devices, per_device(): lax.all_gather(k_mid, 'rail', axis=0, tiled=True)  16.6 us
  transfers between devices with their start and end apart: 9, of which 6 were waited for; matrix products, arithmetic and copies ran while one was open for 18% of the time, Pallas kernels for 0%

commit v1 on v0

v1 whole, which is shorter than its diff:
```python
import functools
import math

import jax
import jax.numpy as jnp
from jax import lax
from jax.experimental import pallas as pl
from jax.experimental.pallas import tpu as pltpu
from jax.sharding import PartitionSpec as P

HEAD = 128
SPAN = 128
NX, NZ, NY, NC = 4, 8, 4, 2
ROWS = 64
BLOCK = NX * ROWS
SLOTS = 4
QHEADS = 4
LANES = QHEADS * SPAN
TILES = 17
CUT = 160
SCALE = 1.0 / math.sqrt(HEAD)
LOG2E = 1.4426950408889634
NEG = -1e30
MESH = pl.DeviceIdType.MESH
F32 = jnp.float32
BF16 = jnp.bfloat16


def halves(lo, hi):
    mid = lo + (hi - lo) // 32 * 16
    return (lo, mid), (mid, hi)


class Place:
    def __init__(self):
        self.x = lax.axis_index("node")
        rail = lax.axis_index("rail")
        self.c = rail % NC
        self.y = (rail // NC) % NY
        self.z = rail // (NC * NY)

    def at(self, x=None, z=None, y=None, c=None):
        x = self.x if x is None else x
        z = self.z if z is None else z
        y = self.y if y is None else y
        c = self.c if c is None else c
        return (x, (z * NY + y) * NC + c)

    def ring(self, axis, step):
        if axis == "z":
            return self.at(z=(self.z + step + NZ) % NZ)
        return self.at(y=(self.y + step + NY) % NY)

    def sibling(self):
        return self.at(c=1 - self.c)

    def team(self):
        out = []
        for step in range(1, NX * NC):
            j = (self.x * NC + self.c + step) % (NX * NC)
            out.append((j, self.at(x=j // NC, c=j % NC)))
        return out


def greet(place):
    barrier = pltpu.get_barrier_semaphore()
    peers = [dev for _, dev in place.team()]
    peers += [place.ring("z", 1), place.ring("z", -1), place.ring("y", 1), place.ring("y", -1)]
    for dev in peers:
        pl.semaphore_signal(barrier, inc=1, device_id=dev, device_id_type=MESH)
    pl.semaphore_wait(barrier, len(peers))


class Copies:
    def __init__(self, send, recv):
        self.send, self.recv, self.count, self.open = send, recv, 0, []

    def make(self, src, dst, dev):
        i = self.count
        self.count += 1
        copy = pltpu.make_async_remote_copy(
            src_ref=src, dst_ref=dst, send_sem=self.send.at[i], recv_sem=self.recv.at[i],
            device_id=dev, device_id_type=MESH,
        )
        copy.start()
        self.open.append(copy)
        return copy

    def finish(self):
        for copy in self.open:
            copy.wait_send()


N_GATHER = 96


def gather_kernel(q_ref, o_ref, k_ref, v_ref, qm_ref, om_ref, kv_ref, send, recv, local):
    me = Place()
    cp = Copies(send, recv)
    greet(me)
    x, z, y, c = me.x, me.z, me.y, me.c
    j_me = x * NC + c
    wide = QHEADS * HEAD

    own = []
    kvx = []
    for step in range(1, NX):
        to = (x + step) % NX
        for i, ref in enumerate((k_ref, v_ref)):
            kvx.append(cp.make(
                ref.at[:, pl.ds(pl.multiple_of(to * HEAD, HEAD), HEAD)],
                kv_ref.at[z, y, c, i, pl.ds(pl.multiple_of(x * ROWS, ROWS), ROWS), :],
                me.at(x=to),
            ))
    for i, ref in enumerate((k_ref, v_ref)):
        own.append(pltpu.make_async_copy(
            ref.at[:, pl.ds(pl.multiple_of(x * HEAD, HEAD), HEAD)],
            kv_ref.at[z, y, c, i, pl.ds(pl.multiple_of(x * ROWS, ROWS), ROWS), :],
            local.at[i],
        ))
        own[-1].start()
    rows = pl.ds(pl.multiple_of(c * BLOCK + x * ROWS, ROWS), ROWS)
    qo = []
    for j, dev in me.team():
        for src, dst in ((q_ref, qm_ref), (o_ref, om_ref)):
            qo.append(cp.make(
                src.at[:, pl.ds(pl.multiple_of(j * wide, wide), wide)], dst.at[rows, :], dev
            ))
    for i, (src, dst) in enumerate(((q_ref, qm_ref), (o_ref, om_ref))):
        own.append(pltpu.make_async_copy(
            src.at[:, pl.ds(pl.multiple_of(j_me * wide, wide), wide)], dst.at[rows, :],
            local.at[2 + i],
        ))
        own[-1].start()
    for copy in kvx:
        copy.wait_recv()
    own[0].wait()
    own[1].wait()

    first = (0, CUT)
    second = (CUT, BLOCK)

    def part(zz, yy, lohi, cc=c):
        lo, hi = lohi
        if yy is None:
            return kv_ref.at[zz, :, cc, :, pl.ds(lo, hi - lo), :]
        return kv_ref.at[zz, yy, cc, :, pl.ds(lo, hi - lo), :]

    def zz(d):
        return (z + d + NZ) % NZ

    def yy(d):
        return (y + d + NY) % NY

    def push(axis, step, zi, yi, lohi):
        ref = part(zi, yi, lohi)
        return cp.make(ref, ref, me.ring(axis, step))

    def y_send(zi, lohi):
        return push("y", 1, zi, y, lohi), push("y", -1, zi, y, lohi)

    def y_forward(zi, lohi, arrivals):
        a, b = halves(*lohi)
        arrivals[0].wait_recv()
        fa = push("y", 1, zi, yy(-1), a)
        arrivals[1].wait_recv()
        fb = push("y", -1, zi, yy(1), b)
        return fa, fb

    sib = []

    def to_sibling(zi, lohi):
        ref = part(zi, None, lohi)
        sib.append(cp.make(ref, ref, me.sibling()))

    def y_finish(zi, lohi, arrivals):
        arrivals[0].wait_recv()
        arrivals[1].wait_recv()
        if lohi is first:
            to_sibling(zi, lohi)

    z1 = push("z", 1, z, y, first), push("z", -1, z, y, first)
    y2 = y_send(z, second)
    stage = [(z, y_send(z, first))]
    y2 = y_forward(z, second, y2)
    y_finish(z, second, y2)
    z2 = push("z", 1, z, None, second), push("z", -1, z, None, second)
    to_sibling(z, second)
    forwarded = []
    for d in range(1, NZ // 2 + 1):
        new = []
        if d < NZ // 2:
            a, b = halves(*first) if d == NZ // 2 - 1 else (first, first)
            z1[0].wait_recv()
            up = push("z", 1, zz(-d), y, a)
            new.append((zz(-d), y_send(zz(-d), first)))
            z1[1].wait_recv()
            down = push("z", -1, zz(d), y, b)
            new.append((zz(d), y_send(zz(d), first)))
            z1 = up, down
        else:
            z1[0].wait_recv()
            z1[1].wait_recv()
            new.append((zz(d), y_send(zz(d), first)))
        done = forwarded
        forwarded = [(zi, y_forward(zi, first, arr)) for zi, arr in stage]
        stage = new
        if d < NZ // 2:
            a, b = halves(*second) if d == NZ // 2 - 1 else (second, second)
            z2[0].wait_recv()
            up = push("z", 1, zz(-d), None, a)
            to_sibling(zz(-d), second)
            z2[1].wait_recv()
            down = push("z", -1, zz(d), None, b)
            to_sibling(zz(d), second)
            z2 = up, down
        for zi, arr in done:
            y_finish(zi, first, arr)
    for zi, arr in forwarded:
        y_finish(zi, first, arr)
    forwarded = [(zi, y_forward(zi, first, arr)) for zi, arr in stage]
    z2[0].wait_recv()
    z2[1].wait_recv()
    to_sibling(zz(NZ // 2), second)
    for zi, arr in forwarded:
        y_finish(zi, first, arr)
    for copy in sib:
        copy.wait_recv()
    for copy in qo:
        copy.wait_recv()
    own[2].wait()
    own[3].wait()
    cp.finish()
    assert cp.count <= N_GATHER


def gather(q, o, k, v):
    wide = QHEADS * HEAD
    any_spec = pl.BlockSpec(memory_space=pl.ANY)
    return pl.pallas_call(
        gather_kernel,
        out_shape=[
            jax.ShapeDtypeStruct((SLOTS * SPAN, wide), BF16),
            jax.ShapeDtypeStruct((SLOTS * SPAN, wide), BF16),
            jax.ShapeDtypeStruct((NZ, NY, NC, 2, BLOCK, HEAD), BF16),
        ],
        in_specs=[any_spec] * 4,
        out_specs=[any_spec] * 3,
        scratch_shapes=[
            pltpu.SemaphoreType.DMA((N_GATHER,)),
            pltpu.SemaphoreType.DMA((N_GATHER,)),
            pltpu.SemaphoreType.DMA((4,)),
        ],
        compiler_params=pltpu.CompilerParams(collective_id=0, has_side_effects=True),
        name="gather",
    )(q, o, k, v)


def attend_kernel(slot_ref, len_ref, q_ref, o_ref, kv_ref, dq_ref, part_ref,
                  qs, os_, s_scr, dp_scr, dqt):
    rail = lax.axis_index("rail")
    chip = rail // NC

    def clear(i, _):
        part_ref[i] = jnp.zeros(part_ref.shape[1:], BF16)
        return 0

    lax.fori_loop(0, part_ref.shape[0], clear, 0)

    lane = lax.broadcasted_iota(jnp.int32, (1, LANES), 1) % SPAN
    sub = lax.broadcasted_iota(jnp.int32, (SPAN, 1), 0)

    def one_slot(s, _):
        def find(i, pos):
            return jnp.where(slot_ref[i] == chip * SLOTS + s, i, pos)

        span = lax.fori_loop(0, NZ * NY * NC * 2, find, 0)
        base = span * SPAN
        rows = pl.ds(pl.multiple_of(s * SPAN, SPAN), SPAN)
        for h in range(QHEADS):
            qs[h * SPAN:(h + 1) * SPAN, :] = q_ref[rows, h * HEAD:(h + 1) * HEAD]
            os_[h * SPAN:(h + 1) * SPAN, :] = o_ref[rows, h * HEAD:(h + 1) * HEAD]

        qpos = base + lane
        qstart = jnp.zeros((1, LANES), jnp.int32)
        start0 = 0
        end = 0
        for i in range(len_ref.shape[0]):
            end = end + len_ref[i]
            qstart = jnp.where(qpos >= end, end, qstart)
            start0 = jnp.where(base >= end, end, start0)
        tiles = span - start0 // SPAN + 1

        def key_slot(t):
            slot = slot_ref[span - t]
            return slot // 2, pl.ds(pl.multiple_of((slot % 2) * SPAN, SPAN), SPAN)

        def first(t, carry):
            m, l = carry
            r, half = key_slot(t)
            st = lax.dot_general(kv_ref[r, 0, half, :], qs[...], (((1,), (1,)), ((), ())),
                                 preferred_element_type=F32) * (SCALE * LOG2E)
            kpos = base - t * SPAN + sub
            st = jnp.where((kpos >= qstart) & (kpos <= qpos), st, NEG)
            s_scr[t] = st
            m_new = jnp.maximum(m, jnp.max(st, axis=0, keepdims=True))
            l = l * jnp.exp2(m - m_new) + jnp.sum(jnp.exp2(st - m_new), axis=0, keepdims=True)
            return m_new, l

        m, l = lax.fori_loop(0, tiles, first,
                             (jnp.full((1, LANES), NEG, F32), jnp.zeros((1, LANES), F32)))
        lse = m + jnp.log2(l)

        def second(t, rd):
            r, half = key_slot(t)
            p = jnp.exp2(s_scr[t] - lse)
            s_scr[t] = p
            dv = jnp.dot(p.astype(BF16), os_[...], preferred_element_type=F32)
            part_ref[r, 1, half, :] = (part_ref[r, 1, half, :].astype(F32) + dv).astype(BF16)
            dp = lax.dot_general(kv_ref[r, 1, half, :], os_[...], (((1,), (1,)), ((), ())),
                                 preferred_element_type=F32)
            dp_scr[t] = dp
            return rd + jnp.sum(p * dp, axis=0, keepdims=True)

        rd = lax.fori_loop(0, tiles, second, jnp.zeros((1, LANES), F32))
        dqt[...] = jnp.zeros_like(dqt)

        def third(t, _):
            r, half = key_slot(t)
            ds = (s_scr[t] * (dp_scr[t] - rd)).astype(BF16)
            dk = jnp.dot(ds, qs[...], preferred_element_type=F32) * SCALE
            part_ref[r, 0, half, :] = (part_ref[r, 0, half, :].astype(F32) + dk).astype(BF16)
            dqt[...] += lax.dot_general(kv_ref[r, 0, half, :], ds, (((0,), (0,)), ((), ())),
                                        preferred_element_type=F32)
            return 0

        lax.fori_loop(0, tiles, third, 0)
        for h in range(QHEADS):
            dq_ref[rows, h * HEAD:(h + 1) * HEAD] = (
                (dqt[:, h * SPAN:(h + 1) * SPAN] * SCALE).T.astype(BF16)
            )
        return 0

    lax.fori_loop(0, SLOTS, one_slot, 0)


def attend(span_slot, doc_lengths, qm, om, kv):
    rails = NZ * NY * NC
    kv = kv.reshape(rails, 2, BLOCK, HEAD)
    smem = pl.BlockSpec(memory_space=pltpu.SMEM)
    vmem = pl.BlockSpec(memory_space=pltpu.VMEM)
    dq, part = pl.pallas_call(
        attend_kernel,
        out_shape=[
            jax.ShapeDtypeStruct(qm.shape, BF16),
            jax.ShapeDtypeStruct(kv.shape, BF16),
        ],
        in_specs=[smem, smem, vmem, vmem, vmem],
        out_specs=[vmem, vmem],
        scratch_shapes=[
            pltpu.VMEM((LANES, HEAD), BF16),
            pltpu.VMEM((LANES, HEAD), BF16),
            pltpu.VMEM((TILES, SPAN, LANES), F32),
            pltpu.VMEM((TILES, SPAN, LANES), F32),
            pltpu.VMEM((HEAD, LANES), F32),
        ],
        compiler_params=pltpu.CompilerParams(vmem_limit_bytes=48 * 1024 * 1024),
        name="attend",
    )(span_slot, doc_lengths, qm, om, kv)
    return dq, part.reshape(NZ, NY, NC, 2, BLOCK, HEAD)


N_SCATTER = 96


def scatter_kernel(dqm_ref, part_ref, dq_ref, dk_ref, dv_ref, acc, sib, yh, yf, z1h, z1f, z2h, z2f,
                   send, recv, local):
    me = Place()
    cp = Copies(send, recv)
    greet(me)
    x, z, y, c = me.x, me.z, me.y, me.c
    j_me = x * NC + c
    wide = QHEADS * HEAD
    D = NZ // 2
    first = (0, CUT)
    second = (CUT, BLOCK)

    def zz(d):
        return (z + d + NZ) % NZ

    def yy(d):
        return (y + d + NY) % NY

    order = [D]
    for d in range(D - 1, 0, -1):
        order += [d, -d]
    order.append(0)
    sibs, owns = {}, {}
    for i, d in enumerate(order):
        sibs[d] = cp.make(part_ref.at[zz(d), :, 1 - c], sib.at[zz(d)], me.sibling())
        owns[d] = pltpu.make_async_copy(part_ref.at[zz(d), :, c], acc.at[zz(d)], local.at[i])
        owns[d].start()
    dqs = []
    for j, dev in me.team():
        dqs.append(cp.make(
            dqm_ref.at[pl.ds(pl.multiple_of((j % NC) * BLOCK + (j // NC) * ROWS, ROWS), ROWS), :],
            dq_ref.at[:, pl.ds(pl.multiple_of(j_me * wide, wide), wide)], dev,
        ))
    dq_own = pltpu.make_async_copy(
        dqm_ref.at[pl.ds(pl.multiple_of(c * BLOCK + x * ROWS, ROWS), ROWS), :],
        dq_ref.at[:, pl.ds(pl.multiple_of(j_me * wide, wide), wide)], local.at[NZ],
    )
    dq_own.start()

    def slab(zi, yi, lohi):
        lo, hi = lohi
        if yi is None:
            return acc.at[zi, :, :, pl.ds(lo, hi - lo), :]
        return acc.at[zi, yi, :, pl.ds(lo, hi - lo), :]

    def add(dst, *srcs):
        total = dst[...].astype(F32)
        for src in srcs:
            total = total + src[...].astype(F32)
        dst[...] = total.astype(BF16)

    def add_planes(zi, lohi, src):
        def body(yi, _):
            add(slab(zi, yi, lohi), src.at[yi])
            return 0
        lax.fori_loop(0, NY, body, 0)

    fa, fb = halves(*first)
    sa, sb = halves(*second)

    def rows_of(ref, lohi):
        return ref.at[:, pl.ds(0, lohi[1] - lohi[0]), :]

    def y1(slot, zi, lohi, ab):
        a, b = ab
        return (
            cp.make(slab(zi, yy(2), a), rows_of(yh.at[slot, 0], a), me.ring("y", 1)),
            cp.make(slab(zi, yy(2), b), rows_of(yh.at[slot, 1], b), me.ring("y", -1)),
        )

    def y2(slot, zi, lohi, ab, arr):
        a, b = ab
        arr[0].wait_recv()
        add(slab(zi, yy(1), a), rows_of(yh.at[slot, 0], a))
        up = cp.make(slab(zi, yy(1), lohi), rows_of(yf.at[slot, 0], lohi), me.ring("y", 1))
        arr[1].wait_recv()
        add(slab(zi, yy(-1), b), rows_of(yh.at[slot, 1], b))
        down = cp.make(slab(zi, yy(-1), lohi), rows_of(yf.at[slot, 1], lohi), me.ring("y", -1))
        return up, down

    def y3(slot, zi, lohi, arr):
        arr[0].wait_recv()
        arr[1].wait_recv()
        add(slab(zi, y, lohi), rows_of(yf.at[slot, 0], lohi), rows_of(yf.at[slot, 1], lohi))

    yarr = {}

    def stage0(i):
        d = order[i]
        owns[d].wait()
        sibs[d].wait_recv()
        add_planes(zz(d), (0, BLOCK), sib.at[zz(d)])
        yarr[d] = y1(i, zz(d), first, (fa, fb))

    def ystep2(i):
        d = order[i]
        yarr[d] = y2(i, zz(d), first, (fa, fb), yarr[d])

    def ystep3(i):
        d = order[i]
        y3(i, zz(d), first, yarr[d])

    def z1_half():
        return (
            cp.make(slab(zz(D), y, fa), rows_of(z1h.at[0], fa), me.ring("z", 1)),
            cp.make(slab(zz(D), y, fb), rows_of(z1h.at[1], fb), me.ring("z", -1)),
        )

    def z2_half():
        return (
            cp.make(slab(zz(D), None, sa), z2h.at[0, :, :, pl.ds(0, sa[1] - sa[0]), :], me.ring("z", 1)),
            cp.make(slab(zz(D), None, sb), z2h.at[1, :, :, pl.ds(0, sb[1] - sb[0]), :], me.ring("z", -1)),
        )

    def z1_step(d, arr):
        a, b = (fa, fb) if d == D - 1 else (first, first)
        src = z1h if d == D - 1 else z1f.at[d]
        arr[0].wait_recv()
        add(slab(zz(d), y, a), rows_of(src.at[0], a))
        up = cp.make(slab(zz(d), y, first), z1f.at[d - 1, 0], me.ring("z", 1))
        arr[1].wait_recv()
        add(slab(zz(-d), y, b), rows_of(src.at[1], b))
        down = cp.make(slab(zz(-d), y, first), z1f.at[d - 1, 1], me.ring("z", -1))
        return up, down

    def z2_step(d, arr):
        a, b = (sa, sb) if d == D - 1 else (second, second)
        src = z2h if d == D - 1 else z2f.at[d]
        arr[0].wait_recv()
        add_planes(zz(d), a, src.at[0, :, :, pl.ds(0, a[1] - a[0]), :])
        up = cp.make(slab(zz(d), None, second), z2f.at[d - 1, 0], me.ring("z", 1))
        arr[1].wait_recv()
        add_planes(zz(-d), b, src.at[1, :, :, pl.ds(0, b[1] - b[0]), :])
        down = cp.make(slab(zz(-d), None, second), z2f.at[d - 1, 1], me.ring("z", -1))
        return up, down

    stage0(0)
    z2 = z2_half()
    stage0(1)
    stage0(2)
    ystep2(0)
    z2 = z2_step(3, z2)
    stage0(3)
    stage0(4)
    ystep3(0)
    z1 = z1_half()
    ystep2(1)
    ystep2(2)
    z2 = z2_step(2, z2)
    stage0(5)
    stage0(6)
    stage0(7)
    ystep3(1)
    ystep3(2)
    z1 = z1_step(3, z1)
    ystep2(3)
    ystep2(4)
    z2 = z2_step(1, z2)
    ystep3(3)
    ystep3(4)
    z1 = z1_step(2, z1)
    ystep2(5)
    ystep2(6)
    ystep2(7)
    z2[0].wait_recv()
    z2[1].wait_recv()
    add_planes(z, second, z2f.at[0, 0])
    add_planes(z, second, z2f.at[0, 1])
    last = y1(NZ, z, second, (sa, sb))
    ystep3(5)
    ystep3(6)
    z1 = z1_step(1, z1)
    last = y2(NZ, z, second, (sa, sb), last)
    ystep3(7)
    y3(NZ, z, second, last)
    z1[0].wait_recv()
    z1[1].wait_recv()
    add(slab(z, y, first), z1f.at[0, 0], z1f.at[0, 1])

    back = []
    mine = pl.ds(pl.multiple_of(x * HEAD, HEAD), HEAD)
    for step in range(1, NX):
        to = (x + step) % NX
        for i, ref in enumerate((dk_ref, dv_ref)):
            back.append(cp.make(
                acc.at[z, y, i, pl.ds(pl.multiple_of(to * ROWS, ROWS), ROWS), :],
                ref.at[:, mine], me.at(x=to),
            ))
    own = []
    for i, ref in enumerate((dk_ref, dv_ref)):
        own.append(pltpu.make_async_copy(
            acc.at[z, y, i, pl.ds(pl.multiple_of(x * ROWS, ROWS), ROWS), :],
            ref.at[:, mine], local.at[NZ + 1 + i],
        ))
        own[-1].start()
    for copy in dqs + back:
        copy.wait_recv()
    dq_own.wait()
    for copy in own:
        copy.wait()
    cp.finish()
    assert cp.count <= N_SCATTER


def scatter(dqm, part):
    any_spec = pl.BlockSpec(memory_space=pl.ANY)
    rest = BLOCK - CUT
    half = max(h[1] - h[0] for h in halves(0, CUT))
    rest_half = max(h[1] - h[0] for h in halves(CUT, BLOCK))
    D = NZ // 2
    return pl.pallas_call(
        scatter_kernel,
        out_shape=[
            jax.ShapeDtypeStruct((ROWS, NX * NC * QHEADS * HEAD), BF16),
            jax.ShapeDtypeStruct((ROWS, NX * HEAD), BF16),
            jax.ShapeDtypeStruct((ROWS, NX * HEAD), BF16),
        ],
        in_specs=[any_spec] * 2,
        out_specs=[any_spec] * 3,
        scratch_shapes=[
            pltpu.VMEM((NZ, NY, 2, BLOCK, HEAD), BF16),
            pltpu.VMEM((NZ, NY, 2, BLOCK, HEAD), BF16),
            pltpu.VMEM((NZ + 1, 2, 2, half, HEAD), BF16),
            pltpu.VMEM((NZ + 1, 2, 2, CUT, HEAD), BF16),
            pltpu.VMEM((2, 2, half, HEAD), BF16),
            pltpu.VMEM((D - 1, 2, 2, CUT, HEAD), BF16),
            pltpu.VMEM((2, NY, 2, rest_half, HEAD), BF16),
            pltpu.VMEM((D - 1, 2, NY, 2, rest, HEAD), BF16),
            pltpu.SemaphoreType.DMA((N_SCATTER,)),
            pltpu.SemaphoreType.DMA((N_SCATTER,)),
            pltpu.SemaphoreType.DMA((NZ + 3,)),
        ],
        compiler_params=pltpu.CompilerParams(
            collective_id=1, has_side_effects=True, vmem_limit_bytes=48 * 1024 * 1024
        ),
        name="scatter",
    )(dqm, part)


def per_device(queries, keys, values, output_cotangent, doc_lengths, span_slot):
    qm, om, kv = gather(queries, output_cotangent, keys, values)
    dqm, part = attend(span_slot, doc_lengths, qm, om, kv)
    return tuple(scatter(dqm, part))


def solution(mesh):
    rows = P(("rail", "node"), None)
    return jax.shard_map(
        per_device, mesh=mesh, in_specs=(rows, rows, rows, rows, P(), P()),
        out_specs=(rows, rows, rows), check_vma=False,
    )
```

time: 604 us -> 145 us (0.24)
  waiting for transfers between devices: 334 us -> 0 us
  Pallas kernels: 0 us -> 138 us
  other arithmetic: 111 us -> 0 us
  local copies, waits for them, and re-layouts: 61.9 us -> 5.44 us
  matrix products: 38.4 us -> 0 us
  starting transfers between devices: 24.3 us -> 0 us
  blocking collectives: 18.2 us -> 0 us
  between operations: 15.4 us -> 0.66 us
    reduce_scatter x2 -> x0, waiting for transfers between devices: 239 us -> none  [the longest x1 147 us: per_device(): lax.psum_scatter(part_values, 'rail', scatter_dimension=0, tiled=True)]
    pallas_call x0 -> x3, Pallas kernels: none -> 138 us  [the longest x1 55.4 us: gather(): pl.pallas_call(gather_kernel, out_shape=[jax.ShapeDtypeStruct((SLOTS * SP...]
    all_gather x2 -> x0, waiting for transfers between devices: 85.7 us -> none  [the longest x1 69.1 us: per_device(): lax.all_gather(v_mid, 'rail', axis=0, tiled=True)]
    scatter-add x4 -> x0, other arithmetic: 76.1 us -> none  [the longest x2 38.1 us: per_device(): part_values.at[rows_both[half_id]].add(value_part.reshape(win_rows, -1))]
    gather x4 -> x0, local copies, waits for them, and re-layouts: 46.7 us -> none  [the longest x2 25.2 us: per_device(): jnp.take(span_slot, clamped // span_rows) * span_rows + clamped % span_rows]
    dot_general x10 -> x0, matrix products: 38.4 us -> none  [the longest x2 11 us: per_device(): jnp.einsum('qhgd,khd->hgqk', grad_blk, value_blk, preferred_element_type=...]
    all_to_all x5 -> x0, starting transfers between devices: 24.2 us -> none  [the longest x1 4.9 us: per_device(): lax.all_to_all(queries, 'node', split_axis=1, concat_axis=0, tiled=True)]
    another operation x4 -> x0, other arithmetic: 20.1 us -> none
  transfers between devices with their start and end apart: 9 -> 0, of which waited for: 6 -> 0; matrix products, arithmetic and copies ran while one was open for 18% -> 0% of each run, Pallas kernels for 0% -> 0%
where the time goes in v1:
time: 145 us; the launch traced here: 144 us
  Pallas kernels  138 us (95%)
  local copies, waits for them, and re-layouts  5.44 us (4%)
    pallas_call x1, Pallas kernels, gather(): pl.pallas_call(gather_kernel, out_shape=[jax.ShapeDtypeStruct((SLOTS * SP...  55.4 us
    pallas_call x1, Pallas kernels, scatter(): pl.pallas_call(scatter_kernel, out_shape=[jax.ShapeDtypeStruct((ROWS, NX...  44.4 us
    pallas_call x1, Pallas kernels, attend(): pl.pallas_call(attend_kernel, out_shape=[jax.ShapeDtypeStruct(qm.shape, B...  38.1 us
    unnamed x11, local copies, waits for them, and re-layouts  5.44 us

profile of v1, /device:TPU:2, one launch (start us, length us, event | category | flops | bytes accessed | tf_op | source)
XLA Modules:
  0.0 144.0 jit_solution(8530449585745539763)
XLA Ops:
  0.6 55.4 %gather.1 = (bf16[512,512]{1,0:T(8,128)(2,1)}, bf16[512,512]{1,0:T(8,128)(2,1)}, bf16[8,4,2,2,256,128]{5,4,3,2,1,0:T(8,128)(2,1)}) custom-call(bf16[64,4096]{1,0:T(8,128)(2,1)} %q_ref.1, bf16[64,4096]{1,0:T(8,128)(2,1)} %o_ref.1, bf16[64,512]{1,0:T(8,128)(2,1)} %k_ref.1, bf16[64,512]{1,0:T(8,128)(2,1)} %v_ref.1), custom_call_target="tpu_custom_call" | custom-call | tf_op jit(solution)/shard_map/gather/pallas_call | solution.py:240
  56.0 0.0 copy-start
  56.0 1.0 copy-done
  57.0 0.0 copy-start.1
  57.1 1.0 copy-done.1
  58.1 0.0 copy-start.2
  58.1 0.7 copy-done.2
  58.7 0.0 copy-start.3
  58.7 0.7 copy-done.3
  59.4 38.1 %attend.1 = (bf16[512,512]{1,0:T(8,128)(2,1)S(1)}, bf16[64,2,256,128]{3,2,1,0:T(8,128)(2,1)}) custom-call(s32[128]{0:T(128)S(1)} %copy-done.2, s32[16]{0:T(128)S(1)} %copy-done.3, bf16[512,512]{1,0:T(8,128)(2,1)S(1)} %copy-done, bf16[512,512]{1,0:T(8,128)(2,1)S(1)} %copy-done.1, bf16[64,2,256,128]{3,2,1,0:T(8,128)(2,1)} %bitcast.2), custom_call_target="tpu_custom_call" | custom-call | tf_op jit(solution)/shard_map/attend/pallas_call | solution.py:352
  97.5 44.4 %scatter.1 = (bf16[64,4096]{1,0:T(8,128)(2,1)S(1)}, bf16[64,512]{1,0:T(8,128)(2,1)S(1)}, bf16[64,512]{1,0:T(8,128)(2,1)S(1)}) custom-call(bf16[512,512]{1,0:T(8,128)(2,1)S(1)} %get-tuple-element.11.dqm_ref, bf16[8,4,2,2,256,128]{5,4,3,2,1,0:T(8,128)(2,1)} %bitcast.3), custom_call_target="tpu_custom_call" | custom-call | tf_op jit(solution)/shard_map/scatter/pallas_call | solution.py:586
  142.0 0.8 copy.12
  142.8 0.6 copy.13
  143.4 0.6 copy.14
Async XLA Ops:
  56.0 1.0 copy-start
  57.0 1.0 copy-start.1
  58.1 0.7 copy-start.2
  58.7 0.7 copy-start.3

commit v2 on v0

v2 whole, which is shorter than its diff:
```python
import math

import jax
import jax.numpy as jnp
from jax import lax
from jax.experimental import pallas as pl
from jax.experimental.pallas import tpu as pltpu
from jax.sharding import PartitionSpec as P

HEAD = 128
SPAN = 128
NX, NZ, NY, NC = 4, 8, 4, 2
ROWS = 64
BLOCK = NX * ROWS
SLOTS = 4
NSLOT = NZ * NY * SLOTS
QHEADS = 4
LANES = QHEADS * SPAN
WIDE = QHEADS * HEAD
STEP = 256
STEPS = 9
WIN = STEP * STEPS
WT = WIN // SPAN
HALF = SPAN // 2
FAR = NZ // 2
SCALE = 1.0 / math.sqrt(HEAD)
C2 = SCALE * 1.4426950408889634
NEG = -1e30
MESH = pl.DeviceIdType.MESH
F32 = jnp.float32
BF16 = jnp.bfloat16
N_SEM = 320
COLUMNS = [0, 1, -1, 2, -2, 3, -3, 4]


class Place:
    def __init__(self):
        self.x = lax.axis_index("node")
        rail = lax.axis_index("rail")
        self.c = rail % NC
        self.y = (rail // NC) % NY
        self.z = rail // (NC * NY)

    def at(self, x=None, z=None, y=None, c=None):
        x = self.x if x is None else x
        z = self.z if z is None else z
        y = self.y if y is None else y
        c = self.c if c is None else c
        return (x, (z * NY + y) * NC + c)

    def zz(self, d):
        return (self.z + d + NZ) % NZ

    def yy(self, d):
        return (self.y + d + NY) % NY

    def ring(self, axis, step):
        return self.at(z=self.zz(step)) if axis == "z" else self.at(y=self.yy(step))

    def sibling(self):
        return self.at(c=1 - self.c)

    def team(self):
        out = []
        for step in range(1, NX * NC):
            j = (self.x * NC + self.c + step) % (NX * NC)
            out.append((j, self.at(x=j // NC, c=j % NC)))
        return out


def greet(place):
    barrier = pltpu.get_barrier_semaphore()
    peers = [dev for _, dev in place.team()]
    peers += [place.ring("z", 1), place.ring("z", -1)]
    peers += [place.ring("y", k) for k in range(1, NY)]
    for dev in peers:
        pl.semaphore_signal(barrier, inc=1, device_id=dev, device_id_type=MESH)
    pl.semaphore_wait(barrier, len(peers))


class Copies:
    def __init__(self, send, recv):
        self.send, self.recv, self.count = send, recv, 0

    def make(self, src, dst, dev):
        i = self.count
        self.count += 1
        return pltpu.make_async_remote_copy(
            src_ref=src, dst_ref=dst, send_sem=self.send.at[i], recv_sem=self.recv.at[i],
            device_id=dev, device_id_type=MESH,
        )


def line(z, c, b):
    return ((z * NC + c) * 2 + b) * NY


class Gather:
    def __init__(self, me, cp, ref):
        self.ref = ref
        c, y = me.c, me.y

        def blk(zi, yi, b, lo=0, n=SPAN):
            return ref.at[line(zi, c, b) + yi, pl.ds(lo, n), :]

        self.z = [{}, {}]
        self.z2 = [[{} for _ in range(NY)] for _ in range(2)]
        for d in range(1, FAR + 1):
            for i, sign in enumerate((1, -1)):
                lo, n = (i * HALF, HALF) if d == FAR else (0, SPAN)
                zi = me.zz(-sign * (d - 1))
                to = me.ring("z", sign)
                src = blk(zi, y, 0, lo, n)
                self.z[i][d] = cp.make(src, src, to)
                for k in range(NY):
                    src = blk(zi, me.yy(k), 1, lo, n)
                    self.z2[i][k][d] = cp.make(src, src, to)
        self.y = {}
        for d in COLUMNS:
            src = blk(me.zz(d), y, 0)
            self.y[d] = [cp.make(src, src, me.ring("y", k)) for k in range(1, NY)]
        src = blk(me.z, y, 1)
        self.y2 = [cp.make(src, src, me.ring("y", k)) for k in range(1, NY)]
        self.sib = [{}, {}]
        for d in COLUMNS:
            for b in range(2):
                src = ref.at[pl.ds(line(me.zz(d), c, b), NY)]
                self.sib[b][d] = cp.make(src, src, me.sibling())

    def begin(self):
        for copy in self.y2:
            copy.start()
        for i in range(2):
            self.z[i][1].start()
        for i in range(2):
            self.z2[i][0][1].start()
        for copy in self.y[0]:
            copy.start()

    def second(self):
        for k in range(1, NY):
            self.y2[k - 1].wait_recv()
            for i in range(2):
                self.z2[i][NY - k][1].start()
        self.sib[1][0].start()

    def zstep(self, d):
        for i, sign in enumerate((1, -1)):
            self.z[i][d].wait_recv()
            if d < FAR:
                self.z[i][d + 1].start()
                for copy in self.y[-sign * d]:
                    copy.start()
        if d == FAR:
            for copy in self.y[FAR]:
                copy.start()
        for k in (0, 3, 2, 1):
            for i in range(2):
                self.z2[i][k][d].wait_recv()
                if d < FAR:
                    self.z2[i][k][d + 1].start()
        self.sib[1][d].start()
        if d < FAR:
            self.sib[1][-d].start()

    def finish(self, *cols):
        for d in cols:
            for copy in self.y[d]:
                copy.wait_recv()
            self.sib[0][d].start()

    def done(self):
        for b in (1, 0):
            for d in COLUMNS:
                self.sib[b][d].wait_recv()

    def drain(self):
        for i in range(2):
            for d in range(1, FAR + 1):
                self.z[i][d].wait_send()
                for k in range(NY):
                    self.z2[i][k][d].wait_send()
        for d in COLUMNS:
            for copy in self.y[d]:
                copy.wait_send()
            for b in range(2):
                self.sib[b][d].wait_send()
        for copy in self.y2:
            copy.wait_send()


def add(dst, *srcs):
    total = dst[...].astype(F32)
    for src in srcs:
        total = total + src[...].astype(F32)
    dst[...] = total.astype(BF16)


class Scatter:
    def __init__(self, me, cp, window, source, bufs):
        self.me, self.window, self.source = me, window, source
        (self.acc, self.snd, self.sibr, self.yr, self.yr1,
         self.zr0h, self.zr0f, self.zr1h, self.zr1f) = bufs
        acc, y = self.acc, me.y
        self.sib, self.y0 = {}, {}
        for i, d in enumerate(COLUMNS):
            self.sib[d] = cp.make(self.snd.at[me.zz(d)], self.sibr.at[me.zz(d)], me.sibling())
            self.y0[d] = [
                cp.make(acc.at[me.zz(d), me.yy(k), 0], self.yr.at[i, k - 1], me.ring("y", k))
                for k in range(1, NY)
            ]
        self.y1 = [cp.make(acc.at[me.z, me.yy(k), 1], self.yr1.at[k - 1], me.ring("y", k))
                   for k in range(1, NY)]
        self.z0 = [{}, {}]
        self.z1 = [[{}, {}], [{}, {}]]
        for d in range(FAR, 0, -1):
            for i, sign in enumerate((1, -1)):
                to = me.ring("z", sign)
                zi = me.zz(sign * d)
                rows = pl.ds(i * HALF, HALF) if d == FAR else pl.ds(0, SPAN)
                dst = self.zr0h.at[i] if d == FAR else self.zr0f.at[d - 1, i]
                self.z0[i][d] = cp.make(acc.at[zi, y, 0, rows, :], dst, to)
                for h in range(2):
                    ys = pl.ds(2 * h, 2)
                    dst = self.zr1h.at[i, ys] if d == FAR else self.zr1f.at[d - 1, i, ys]
                    self.z1[i][h][d] = cp.make(acc.at[zi, ys, 1, rows, :], dst, to)

    def drain(self):
        for d in COLUMNS:
            self.sib[d].wait_send()
            for copy in self.y0[d]:
                copy.wait_send()
        for copy in self.y1:
            copy.wait_send()
        for i in range(2):
            for d in range(1, FAR + 1):
                self.z0[i][d].wait_send()
                for h in range(2):
                    self.z1[i][h][d].wait_send()

    def collect(self, d):
        me = self.me
        zi = me.zz(d)

        def tiles(core, dst):
            def body(i, _):
                yi, b = i // 2, i % 2
                j = line(zi, core, b) + yi
                total = None
                for s in range(SLOTS):
                    w = self.source[s * NSLOT + j]
                    tile = self.window[w]
                    total = tile if total is None else total + tile
                dst[zi, yi, b] = total
                return 0
            lax.fori_loop(0, NY * 2, body, 0, unroll=4)

        tiles(1 - me.c, self.snd)
        self.sib[d].start()
        tiles(me.c, self.acc)

    def pair(self, *cols):
        me = self.me
        for d in cols:
            zi = me.zz(d)
            self.sib[d].wait_recv()

            def body(yi, _):
                add(self.acc.at[zi, yi], self.sibr.at[zi, yi])
                return 0

            lax.fori_loop(0, NY, body, 0)
            for copy in self.y0[d]:
                copy.start()
            if d == FAR:
                for h in range(2):
                    for i in range(2):
                        self.z1[i][h][d].start()

    def yadd(self, *cols):
        me = self.me
        for d in cols:
            j = COLUMNS.index(d)
            for copy in self.y0[d]:
                copy.wait_recv()
            add(self.acc.at[me.zz(d), me.y, 0], *[self.yr.at[j, k] for k in range(NY - 1)])
            if d == FAR:
                for i in range(2):
                    self.z0[i][d].start()

    def z0step(self, d):
        me = self.me
        for i, sign in enumerate((1, -1)):
            self.z0[i][d + 1].wait_recv()
            zi = me.zz(sign * d)
            if d == FAR - 1:
                add(self.acc.at[zi, me.y, 0, pl.ds(i * HALF, HALF), :], self.zr0h.at[i])
            else:
                add(self.acc.at[zi, me.y, 0], self.zr0f.at[d, i])
            self.z0[i][d].start()

    def z1step(self, d):
        me = self.me
        for h in range(2):
            for i, sign in enumerate((1, -1)):
                self.z1[i][h][d + 1].wait_recv()
                zi = me.zz(sign * d)
                for yi in range(2 * h, 2 * h + 2):
                    if d == FAR - 1:
                        add(self.acc.at[zi, yi, 1, pl.ds(i * HALF, HALF), :], self.zr1h.at[i, yi])
                    else:
                        add(self.acc.at[zi, yi, 1], self.zr1f.at[d, i, yi])
                self.z1[i][h][d].start()

    def z1last(self):
        me = self.me
        for h in range(2):
            for i in range(2):
                self.z1[i][h][1].wait_recv()
            for yi in range(2 * h, 2 * h + 2):
                add(self.acc.at[me.z, yi, 1], self.zr1f.at[0, 0, yi], self.zr1f.at[0, 1, yi])
        for copy in self.y1:
            copy.start()

    def z0last(self):
        me = self.me
        for i in range(2):
            self.z0[i][1].wait_recv()
        add(self.acc.at[me.z, me.y, 0], self.zr0f.at[0, 0], self.zr0f.at[0, 1])

    def y1last(self):
        me = self.me
        for copy in self.y1:
            copy.wait_recv()
        add(self.acc.at[me.z, me.y, 1], *[self.yr1.at[k] for k in range(NY - 1)])


def fold(x, op):
    return op(x.reshape(x.shape[0] // 8, 8, x.shape[1]), axis=0)


def at_step(t):
    return pl.ds(t * STEP, STEP)


def span_rows(i):
    return pl.ds(pl.multiple_of(i * SPAN, SPAN), SPAN)


def load_window(s, seen, src, put):
    def body(w, _):
        j = seen[s * WT + w]
        put(w, src[j])
        return 0

    lax.fori_loop(0, WT, body, 0, unroll=2)


def tables_kernel(slot_ref, len_ref, seen, source, rows_ref, span_of):
    chip = lax.axis_index("rail") // NC
    lane = lax.broadcasted_iota(jnp.int32, (1, LANES), 1) % SPAN

    def invert(i, _):
        span_of[slot_ref[i]] = i
        return 0

    lax.fori_loop(0, NSLOT, invert, 0, unroll=8)

    for s in range(SLOTS):
        def clear(i, _):
            source[s * NSLOT + i] = s * WT
            return 0

        lax.fori_loop(0, NSLOT, clear, 0, unroll=8)
        span = span_of[chip * SLOTS + s]
        seen[s * WT] = 0

        def fill(w, _):
            n = span - (WT - 1) + w
            j = slot_ref[jnp.maximum(n, 0)]
            j = (j // 16) * 16 + (j % 4) * 4 + (j // 4) % 4
            seen[s * WT + w] = j

            @pl.when(n >= 0)
            def _():
                source[s * NSLOT + j] = s * WT + w

            return 0

        lax.fori_loop(1, WT, fill, 0)
        qpos = span * SPAN + lane
        qstart = jnp.zeros((1, LANES), jnp.int32)
        end = 0
        for i in range(len_ref.shape[0]):
            end = end + len_ref[i]
            qstart = jnp.where(qpos >= end, end, qstart)
        rows_ref[s, 0:1, :] = qstart - (span - (WT - 1)) * SPAN
        rows_ref[s, 1:2, :] = qpos - qstart


def kernel(seen, source, rows_ref, q_ref, o_ref, k_ref, v_ref, dq_ref, dk_ref, dv_ref,
           k_all, v_all, qm, om, kw, vw, qs, os_, tq, s_scr, p_scr, wk, wv, inv_scr, dqt, dqm,
           *rest):
    bufs_v, bufs_k = rest[:9], rest[9:18]
    send, recv, local = rest[18:]
    me = Place()
    cp = Copies(send, recv)
    x, z, y, c = me.x, me.z, me.y, me.c
    j_me = x * NC + c

    def cols(j, n):
        return pl.ds(pl.multiple_of(j * n, n), n)

    kvx = [[], []]
    own = []
    mine = pl.ds(pl.multiple_of((x % 2) * ROWS, ROWS), ROWS)
    for i, (src, dst) in enumerate(((k_ref, k_all), (v_ref, v_all))):
        for step in range(1, NX):
            to = (x + step) % NX
            kvx[i].append(cp.make(
                src.at[:, cols(to, HEAD)], dst.at[line(z, c, x // 2) + y, mine, :], me.at(x=to)))
        own.append(pltpu.make_async_copy(
            src.at[:, cols(x, HEAD)], dst.at[line(z, c, x // 2) + y, mine, :], local.at[i]))
    rows = pl.ds(pl.multiple_of(c * BLOCK + x * ROWS, ROWS), ROWS)
    qo = []
    for j, dev in me.team():
        for src, dst in ((q_ref, qm), (o_ref, om)):
            qo.append(cp.make(src.at[:, cols(j, WIDE)], dst.at[rows, :], dev))
    for i, (src, dst) in enumerate(((q_ref, qm), (o_ref, om))):
        own.append(pltpu.make_async_copy(
            src.at[:, cols(j_me, WIDE)], dst.at[rows, :], local.at[2 + i]))
    gk, gv = Gather(me, cp, k_all), Gather(me, cp, v_all)
    sv = Scatter(me, cp, wv, source, bufs_v)
    sk = Scatter(me, cp, wk, source, bufs_k)
    dqs = []
    for j, dev in me.team():
        there = pl.ds(pl.multiple_of((j % NC) * BLOCK + (j // NC) * ROWS, ROWS), ROWS)
        dqs.append(cp.make(dqm.at[there, :], dq_ref.at[:, cols(j_me, WIDE)], dev))
    own.append(pltpu.make_async_copy(dqm.at[rows, :], dq_ref.at[:, cols(j_me, WIDE)], local.at[4]))
    back = [[], []]
    for i, (acc, dst) in enumerate(((bufs_k[0], dk_ref), (bufs_v[0], dv_ref))):
        for step in range(1, NX):
            to = (x + step) % NX
            part = pl.ds(pl.multiple_of((to % 2) * ROWS, ROWS), ROWS)
            back[i].append(cp.make(
                acc.at[z, y, to // 2, part, :], dst.at[:, cols(x, HEAD)], me.at(x=to)))
        own.append(pltpu.make_async_copy(
            acc.at[z, y, x // 2, mine, :], dst.at[:, cols(x, HEAD)], local.at[5 + i]))
    assert cp.count <= N_SEM

    greet(me)
    for i in range(2):
        for copy in kvx[i]:
            copy.start()
        own[i].start()
    for copy in qo:
        copy.start()
    own[2].start()
    own[3].start()

    for copy in kvx[0]:
        copy.wait_recv()
    own[0].wait()
    gk.begin()
    gk.second()
    for copy in kvx[1]:
        copy.wait_recv()
    own[1].wait()
    gv.begin()
    gk.zstep(1)
    gk.finish(0)
    gv.second()
    gk.zstep(2)
    gk.finish(1, -1)
    gk.zstep(3)
    gv.zstep(1)
    gk.finish(2, -2)
    gk.zstep(4)
    gk.finish(3, -3)
    gv.finish(0)
    gv.zstep(2)
    gk.finish(4)
    gk.done()
    for copy in qo:
        copy.wait_recv()
    own[2].wait()
    own[3].wait()

    sub = lax.broadcasted_iota(jnp.int32, (STEP, 1), 0)

    def during(s, table):
        for i, events in enumerate(table):
            if events:
                @pl.when(s == i)
                def _():
                    for event in events:
                        event()

    def first_part(s, _):
        low, extra = rows_ref[s, 0:1, :], rows_ref[s, 1:2, :]

        def put(w, tile):
            kw[s, span_rows(w), :] = tile

        load_window(s, seen, k_all, put)
        for h in range(QHEADS):
            qh = qm[span_rows(s), h * HEAD:(h + 1) * HEAD]
            qs[s, h * SPAN:(h + 1) * SPAN, :] = qh
            tq[:, h * SPAN:(h + 1) * SPAN] = qh.T
        top = jnp.full((8, LANES), NEG, F32)
        for t in range(STEPS):
            st = jnp.dot(kw[s, at_step(t), :], tq[...], preferred_element_type=F32)
            rel = (sub + t * STEP) - low
            st = jnp.where((rel >= 0) & (rel <= extra), st, NEG)
            s_scr[t] = st
            top = jnp.maximum(top, fold(st, jnp.max))
        during(s, v_events[0])
        mc = jnp.max(top, axis=0, keepdims=True) * C2
        total = jnp.zeros((8, LANES), F32)
        for t in range(STEPS):
            p = jnp.exp2(s_scr[t] * C2 - mc)
            p_scr[s, t] = p.astype(BF16)
            total = total + fold(p, jnp.sum)
        inv = 1.0 / jnp.sum(total, axis=0, keepdims=True)
        inv8 = jnp.broadcast_to(inv, (8, LANES))
        inv_scr[s] = inv8
        for h in range(QHEADS):
            col = inv8[:, h * SPAN:(h + 1) * SPAN].T[:, :1]
            oh = om[span_rows(s), h * HEAD:(h + 1) * HEAD].astype(F32)
            os_[s, h * SPAN:(h + 1) * SPAN, :] = (oh * col).astype(BF16)
        during(s, v_events[1])
        for t in range(STEPS):
            dv = jnp.dot(p_scr[s, t], os_[s], preferred_element_type=F32)
            wv[pl.ds(s * WT + 2 * t, 2)] = dv.astype(BF16).reshape(2, SPAN, HEAD)
        during(s, v_events[2])
        return 0

    v_events = [
        [[lambda: gv.finish(1, -1)], [lambda: gv.zstep(4)], [lambda: gv.finish(3, -3)], None],
        [None, None, None, None],
        [[lambda: gv.zstep(3)], [lambda: gv.finish(2, -2)], [lambda: gv.finish(4)], None],
    ]
    lax.fori_loop(0, SLOTS, first_part, 0)
    gv.done()

    sv.collect(4)
    sv.collect(3)
    sv.collect(-3)
    sv.pair(4)
    sv.pair(3, -3)

    def second_part(s, _):

        def put(w, tile):
            vw[span_rows(w), :] = tile

        load_window(s, seen, v_all, put)
        for h in range(QHEADS):
            tq[:, h * SPAN:(h + 1) * SPAN] = os_[s, h * SPAN:(h + 1) * SPAN, :].T
        total = jnp.zeros((8, LANES), F32)
        for t in range(STEPS):
            dp = jnp.dot(vw[at_step(t), :], tq[...], preferred_element_type=F32)
            s_scr[t] = dp
            total = total + fold(p_scr[s, t].astype(F32) * dp, jnp.sum)
        during(s, k_events[0])
        dots = jnp.sum(total, axis=0, keepdims=True) * inv_scr[s, :1, :]
        dqt[...] = jnp.zeros_like(dqt)
        for t in range(STEPS):
            ds = (p_scr[s, t].astype(F32) * (s_scr[t] - dots)).astype(BF16)
            dk = jnp.dot(ds, qs[s], preferred_element_type=F32) * SCALE
            wk[pl.ds(s * WT + 2 * t, 2)] = dk.astype(BF16).reshape(2, SPAN, HEAD)
            dqt[...] += lax.dot_general(kw[s, at_step(t), :], ds, (((0,), (0,)), ((), ())),
                                        preferred_element_type=F32)
        for h in range(QHEADS):
            dqm[span_rows(s), h * HEAD:(h + 1) * HEAD] = (
                (dqt[:, h * SPAN:(h + 1) * SPAN] * SCALE).T.astype(BF16))
        during(s, k_events[1])
        return 0

    k_events = [
        [
            [lambda: sv.collect(2), lambda: sv.collect(-2)],
            [lambda: sv.collect(1), lambda: sv.collect(-1), lambda: sv.z1step(2)],
            [lambda: sv.collect(0), lambda: sv.pair(1, -1)],
            [lambda: sv.z0step(2), lambda: sv.z1step(1)],
        ],
        [
            [lambda: sv.z1step(3), lambda: sv.pair(2, -2), lambda: sv.yadd(4)],
            [lambda: sv.yadd(3, -3), lambda: sv.z0step(3)],
            [lambda: sv.yadd(2, -2), lambda: sv.pair(0)],
            [lambda: sv.yadd(1, -1)],
        ],
    ]
    lax.fori_loop(0, SLOTS, second_part, 0)
    for copy in dqs:
        copy.start()
    own[4].start()

    sk.collect(4)
    sv.z0step(1)
    sk.collect(3)
    sk.collect(-3)
    sk.pair(4)
    sv.z1last()
    sk.collect(2)
    sk.collect(-2)
    sk.pair(3, -3)
    sv.yadd(0)
    sk.yadd(4)
    sk.collect(1)
    sk.collect(-1)
    sk.z1step(3)
    sk.pair(2, -2)
    sv.z0last()
    sk.yadd(3, -3)
    sk.z0step(3)
    sk.collect(0)
    sv.y1last()
    for copy in back[1]:
        copy.start()
    own[6].start()
    sk.pair(1, -1)
    sk.pair(0)
    sk.z1step(2)
    sk.yadd(2, -2)
    sk.z0step(2)
    sk.yadd(1, -1)
    gk.drain()
    sk.z1step(1)
    sk.z0step(1)
    sk.yadd(0)
    gv.drain()
    sk.z1last()
    for copy in kvx[0] + kvx[1] + qo:
        copy.wait_send()
    sk.z0last()
    sv.drain()
    sk.y1last()
    for copy in back[0]:
        copy.start()
    own[5].start()
    sk.drain()
    for copy in dqs + back[1] + back[0]:
        copy.wait_recv()
        copy.wait_send()
    for i in (4, 5, 6):
        own[i].wait()


def per_device(queries, keys, values, output_cotangent, doc_lengths, span_slot):
    smem = pl.BlockSpec(memory_space=pltpu.SMEM)
    any_spec = pl.BlockSpec(memory_space=pl.ANY)

    def vmem(*shape, dtype=BF16):
        return pltpu.VMEM(shape, dtype)

    scatter_bufs = [
        vmem(NZ, NY, 2, SPAN, HEAD),
        vmem(NZ, NY, 2, SPAN, HEAD),
        vmem(NZ, NY, 2, SPAN, HEAD),
        vmem(NZ, NY - 1, SPAN, HEAD),
        vmem(NY - 1, SPAN, HEAD),
        vmem(2, HALF, HEAD),
        vmem(FAR - 1, 2, SPAN, HEAD),
        vmem(2, NY, HALF, HEAD),
        vmem(FAR - 1, 2, NY, SPAN, HEAD),
    ]
    seen, source, rows = pl.pallas_call(
        tables_kernel,
        out_shape=[
            jax.ShapeDtypeStruct((SLOTS * WT,), jnp.int32),
            jax.ShapeDtypeStruct((SLOTS * NSLOT,), jnp.int32),
            jax.ShapeDtypeStruct((SLOTS, 8, LANES), jnp.int32),
        ],
        in_specs=[smem] * 2,
        out_specs=[smem, smem, pl.BlockSpec(memory_space=pltpu.VMEM)],
        scratch_shapes=[pltpu.SMEM((NSLOT,), jnp.int32)],
        name="tables",
    )(span_slot, doc_lengths)
    outs = pl.pallas_call(
        kernel,
        out_shape=[
            jax.ShapeDtypeStruct(queries.shape, BF16),
            jax.ShapeDtypeStruct(keys.shape, BF16),
            jax.ShapeDtypeStruct(values.shape, BF16),
        ],
        in_specs=[smem] * 2 + [pl.BlockSpec(memory_space=pltpu.VMEM)] + [any_spec] * 4,
        out_specs=[any_spec] * 3,
        scratch_shapes=[
            vmem(NSLOT, SPAN, HEAD),
            vmem(NSLOT, SPAN, HEAD),
            vmem(SLOTS * SPAN, WIDE),
            vmem(SLOTS * SPAN, WIDE),
            vmem(SLOTS, WIN, HEAD),
            vmem(WIN, HEAD),
            vmem(SLOTS, LANES, HEAD),
            vmem(SLOTS, LANES, HEAD),
            vmem(HEAD, LANES),
            vmem(STEPS, STEP, LANES, dtype=F32),
            vmem(SLOTS, STEPS, STEP, LANES),
            vmem(SLOTS * WT, SPAN, HEAD),
            vmem(SLOTS * WT, SPAN, HEAD),
            vmem(SLOTS, 8, LANES, dtype=F32),
            vmem(HEAD, LANES, dtype=F32),
            vmem(SLOTS * SPAN, WIDE),
        ] + scatter_bufs * 2 + [
            pltpu.SemaphoreType.DMA((N_SEM,)),
            pltpu.SemaphoreType.DMA((N_SEM,)),
            pltpu.SemaphoreType.DMA((8,)),
        ],
        compiler_params=pltpu.CompilerParams(
            collective_id=0, has_side_effects=True, vmem_limit_bytes=60 * 1024 * 1024),
        name="attention_backward",
    )(seen, source, rows, queries, output_cotangent, keys, values)
    return tuple(outs)


def solution(mesh):
    rows = P(("rail", "node"), None)
    return jax.shard_map(
        per_device, mesh=mesh, in_specs=(rows, rows, rows, rows, P(), P()),
        out_specs=(rows, rows, rows), check_vma=False,
    )
```

time: 604 us -> 117 us (0.19)
  waiting for transfers between devices: 334 us -> 0 us
  Pallas kernels: 0 us -> 112 us
  other arithmetic: 111 us -> 0 us
  local copies, waits for them, and re-layouts: 61.9 us -> 3.4 us
  matrix products: 38.4 us -> 0 us
  starting transfers between devices: 24.3 us -> 0 us
  blocking collectives: 18.2 us -> 0 us
  between operations: 15.4 us -> 0.66 us
    reduce_scatter x2 -> x0, waiting for transfers between devices: 239 us -> none  [the longest x1 147 us: per_device(): lax.psum_scatter(part_values, 'rail', scatter_dimension=0, tiled=True)]
    pallas_call x0 -> x2, Pallas kernels: none -> 112 us  [the longest x1 108 us: per_device(): pl.pallas_call(kernel, out_shape=[jax.ShapeDtypeStruct(queries.shape, BF1...]
    all_gather x2 -> x0, waiting for transfers between devices: 85.7 us -> none  [the longest x1 69.1 us: per_device(): lax.all_gather(v_mid, 'rail', axis=0, tiled=True)]
    scatter-add x4 -> x0, other arithmetic: 76.1 us -> none  [the longest x2 38.1 us: per_device(): part_values.at[rows_both[half_id]].add(value_part.reshape(win_rows, -1))]
    gather x4 -> x0, local copies, waits for them, and re-layouts: 46.7 us -> none  [the longest x2 25.2 us: per_device(): jnp.take(span_slot, clamped // span_rows) * span_rows + clamped % span_rows]
    dot_general x10 -> x0, matrix products: 38.4 us -> none  [the longest x2 11 us: per_device(): jnp.einsum('qhgd,khd->hgqk', grad_blk, value_blk, preferred_element_type=...]
    all_to_all x5 -> x0, starting transfers between devices: 24.2 us -> none  [the longest x1 4.9 us: per_device(): lax.all_to_all(queries, 'node', split_axis=1, concat_axis=0, tiled=True)]
    another operation x4 -> x0, other arithmetic: 20.1 us -> none
  transfers between devices with their start and end apart: 9 -> 0, of which waited for: 6 -> 0; matrix products, arithmetic and copies ran while one was open for 18% -> 0% of each run, Pallas kernels for 0% -> 0%
where the time goes in v2:
time: 117 us; the launch traced here: 116 us
  Pallas kernels  112 us (96%)
  local copies, waits for them, and re-layouts  3.4 us (3%)
    pallas_call x1, Pallas kernels, per_device(): pl.pallas_call(kernel, out_shape=[jax.ShapeDtypeStruct(queries.shape, BF1...  108 us
    pallas_call x1, Pallas kernels, per_device(): pl.pallas_call(tables_kernel, out_shape=[jax.ShapeDtypeStruct((SLOTS * WT...  3.86 us
    unnamed x7, local copies, waits for them, and re-layouts  3.4 us

profile of v2, /device:TPU:2, one launch (start us, length us, event | category | flops | bytes accessed | tf_op | source)
XLA Modules:
  0.0 116.4 jit_solution(7789595445066639471)
XLA Ops:
  0.6 3.9 %tables.1 = (s32[72]{0:T(128)}, s32[512]{0:T(512)}, s32[4,8,512]{2,1,0:T(8,128)}) custom-call(s32[128]{0:T(128)} %slot_ref.1, s32[16]{0:T(128)} %len_ref.1), custom_call_target="tpu_custom_call" | custom-call | tf_op jit(solution)/shard_map/tables/pallas_call | solution.py:668
  4.5 108.5 %attention_backward.1 = (bf16[64,4096]{1,0:T(8,128)(2,1)}, bf16[64,512]{1,0:T(8,128)(2,1)}, bf16[64,512]{1,0:T(8,128)(2,1)}) custom-call(s32[72]{0:T(128)} %get-tuple-element.6.seen, s32[512]{0:T(512)} %get-tuple-element.7.source, s32[4,8,512]{2,1,0:T(8,128)} %get-tuple-element.8.rows_ref, bf16[64,4096]{1,0:T(8,128)(2,1)} %q_ref.1, bf16[64,4096]{1,0:T(8,128)(2,1)} %o_ref.1, ...), custom_call_target="tpu_custom_call" | custom-call | tf_op jit(solution)/shard_map/attention_backward/pallas_call | solution.py:680
  113.0 0.0 copy-start.1
  113.0 1.9 %copy.12 = bf16[64,4096]{1,0:T(8,128)(2,1)} copy(bf16[64,4096]{1,0:T(8,128)(2,1)} %get-tuple-element.12) | data formatting | bytes 1048576
  114.9 0.0 copy-done.1
  114.9 0.0 copy-start
  114.9 0.6 copy.13
  115.5 0.2 copy-done
  115.8 0.6 copy.14
Async XLA Ops:
  113.0 1.9 %copy-start.1 = (bf16[64,512]{1,0:T(8,128)(2,1)S(1)}, bf16[64,512]{1,0:T(8,128)(2,1)}, u32[]{:S(2)}) copy-start(bf16[64,512]{1,0:T(8,128)(2,1)} %get-tuple-element.13) | copy-start | bytes 196612
  114.9 0.9 copy-start

commit v3 on v2

--- a/solution.py
+++ b/solution.py
@@ -29,7 +29,9 @@
 MESH = pl.DeviceIdType.MESH
 F32 = jnp.float32
 BF16 = jnp.bfloat16
-N_SEM = 320
+N_RECV = 208
+N_SEND = 5
+RULER = 126
 COLUMNS = [0, 1, -1, 2, -2, 3, -3, 4]
 
 
@@ -79,29 +81,46 @@
 
 
 class Copies:
-    def __init__(self, send, recv):
-        self.send, self.recv, self.count = send, recv, 0
-
-    def make(self, src, dst, dev):
-        i = self.count
+    def __init__(self, send, recv, ruler):
+        self.send, self.recv, self.ruler, self.count = send, recv, ruler, 0
+
+    def slot(self):
         self.count += 1
+        return self.count - 1
+
+    def make(self, src, dst, dev, group, slot=None):
+        slot = self.slot() if slot is None else slot
         return pltpu.make_async_remote_copy(
-            src_ref=src, dst_ref=dst, send_sem=self.send.at[i], recv_sem=self.recv.at[i],
+            src_ref=src, dst_ref=dst, send_sem=self.send.at[group], recv_sem=self.recv.at[slot],
             device_id=dev, device_id_type=MESH,
         )
 
+    def size(self, spans, rows=SPAN):
+        return self.ruler.at[pl.ds(0, spans), pl.ds(0, rows), :]
+
+    def arrived(self, slot, spans, rows=SPAN):
+        ref = self.size(spans, rows)
+        pltpu.make_async_copy(ref, ref, self.recv.at[slot]).wait()
+
+    def sent(self, group, spans):
+        ref = self.size(spans)
+        pltpu.make_async_copy(ref, ref, self.send.at[group]).wait()
+
 
 def line(z, c, b):
     return ((z * NC + c) * 2 + b) * NY
 
 
 class Gather:
-    def __init__(self, me, cp, ref):
-        self.ref = ref
+    def __init__(self, me, cp, ref, group):
+        self.cp, self.ref, self.group = cp, ref, group
         c, y = me.c, me.y
 
         def blk(zi, yi, b, lo=0, n=SPAN):
             return ref.at[line(zi, c, b) + yi, pl.ds(lo, n), :]
+
+        def make(src, dev, slot=None):
+            return cp.make(src, src, dev, group, slot)
 
         self.z = [{}, {}]
         self.z2 = [[{} for _ in range(NY)] for _ in range(2)]
@@ -110,28 +129,28 @@
                 lo, n = (i * HALF, HALF) if d == FAR else (0, SPAN)
                 zi = me.zz(-sign * (d - 1))
                 to = me.ring("z", sign)
-                src = blk(zi, y, 0, lo, n)
-                self.z[i][d] = cp.make(src, src, to)
+                self.z[i][d] = make(blk(zi, y, 0, lo, n), to)
                 for k in range(NY):
-                    src = blk(zi, me.yy(k), 1, lo, n)
-                    self.z2[i][k][d] = cp.make(src, src, to)
-        self.y = {}
+                    self.z2[i][k][d] = make(blk(zi, me.yy(k), 1, lo, n), to)
+        self.y, self.y_slot = {}, {}
         for d in COLUMNS:
+            self.y_slot[d] = cp.slot()
             src = blk(me.zz(d), y, 0)
-            self.y[d] = [cp.make(src, src, me.ring("y", k)) for k in range(1, NY)]
+            self.y[d] = [make(src, me.ring("y", k), self.y_slot[d]) for k in range(1, NY)]
         src = blk(me.z, y, 1)
-        self.y2 = [cp.make(src, src, me.ring("y", k)) for k in range(1, NY)]
+        self.y2 = [make(src, me.ring("y", k)) for k in range(1, NY)]
         self.sib = [{}, {}]
+        self.sib_slot = cp.slot()
         for d in COLUMNS:
             for b in range(2):
                 src = ref.at[pl.ds(line(me.zz(d), c, b), NY)]
-                self.sib[b][d] = cp.make(src, src, me.sibling())
+                self.sib[b][d] = make(src, me.sibling(), self.sib_slot)
 
     def begin(self):
+        for i in range(2):
+            self.z[i][1].start()
         for copy in self.y2:
             copy.start()
-        for i in range(2):
-            self.z[i][1].start()
         for i in range(2):
             self.z2[i][0][1].start()
         for copy in self.y[0]:
@@ -144,7 +163,7 @@
                 self.z2[i][NY - k][1].start()
         self.sib[1][0].start()
 
-    def zstep(self, d):
+    def near(self, d):
         for i, sign in enumerate((1, -1)):
             self.z[i][d].wait_recv()
             if d < FAR:
@@ -154,6 +173,8 @@
         if d == FAR:
             for copy in self.y[FAR]:
                 copy.start()
+
+    def wide(self, d):
         for k in (0, 3, 2, 1):
             for i in range(2):
                 self.z2[i][k][d].wait_recv()
@@ -165,28 +186,14 @@
 
     def finish(self, *cols):
         for d in cols:
-            for copy in self.y[d]:
-                copy.wait_recv()
+            self.cp.arrived(self.y_slot[d], NY - 1)
             self.sib[0][d].start()
 
     def done(self):
-        for b in (1, 0):
-            for d in COLUMNS:
-                self.sib[b][d].wait_recv()
+        self.cp.arrived(self.sib_slot, NSLOT // 2)
 
     def drain(self):
-        for i in range(2):
-            for d in range(1, FAR + 1):
-                self.z[i][d].wait_send()
-                for k in range(NY):
-                    self.z2[i][k][d].wait_send()
-        for d in COLUMNS:
-            for copy in self.y[d]:
-                copy.wait_send()
-            for b in range(2):
-                self.sib[b][d].wait_send()
-        for copy in self.y2:
-            copy.wait_send()
+        self.cp.sent(self.group, RULER)
 
 
 def add(dst, *srcs):
@@ -197,20 +204,29 @@
 
 
 class Scatter:
-    def __init__(self, me, cp, window, source, bufs):
-        self.me, self.window, self.source = me, window, source
+    def __init__(self, me, cp, window, source, bufs, group):
+        self.me, self.cp, self.window, self.source, self.group = me, cp, window, source, group
         (self.acc, self.snd, self.sibr, self.yr, self.yr1,
          self.zr0h, self.zr0f, self.zr1h, self.zr1f) = bufs
         acc, y = self.acc, me.y
-        self.sib, self.y0 = {}, {}
+        self.sib, self.y0, self.y0_slot = {}, {}, {}
+
+        def make(src, dst, dev, slot=None):
+            return cp.make(src, dst, dev, group, slot)
+
         for i, d in enumerate(COLUMNS):
-            self.sib[d] = cp.make(self.snd.at[me.zz(d)], self.sibr.at[me.zz(d)], me.sibling())
+            self.sib[d] = make(self.snd.at[me.zz(d)], self.sibr.at[me.zz(d)], me.sibling())
+            self.y0_slot[d] = cp.slot()
             self.y0[d] = [
-                cp.make(acc.at[me.zz(d), me.yy(k), 0], self.yr.at[i, k - 1], me.ring("y", k))
+                make(acc.at[me.zz(d), me.yy(k), 0], self.yr.at[i, k - 1], me.ring("y", k),
+                     self.y0_slot[d])
                 for k in range(1, NY)
             ]
-        self.y1 = [cp.make(acc.at[me.z, me.yy(k), 1], self.yr1.at[k - 1], me.ring("y", k))
-                   for k in range(1, NY)]
+        self.y1_slot = cp.slot()
+        self.y1 = [
+            make(acc.at[me.z, me.yy(k), 1], self.yr1.at[k - 1], me.ring("y", k), self.y1_slot)
+            for k in range(1, NY)
+        ]
         self.z0 = [{}, {}]
         self.z1 = [[{}, {}], [{}, {}]]
         for d in range(FAR, 0, -1):
@@ -219,24 +235,14 @@
                 zi = me.zz(sign * d)
                 rows = pl.ds(i * HALF, HALF) if d == FAR else pl.ds(0, SPAN)
                 dst = self.zr0h.at[i] if d == FAR else self.zr0f.at[d - 1, i]
-                self.z0[i][d] = cp.make(acc.at[zi, y, 0, rows, :], dst, to)
+                self.z0[i][d] = make(acc.at[zi, y, 0, rows, :], dst, to)
                 for h in range(2):
                     ys = pl.ds(2 * h, 2)
                     dst = self.zr1h.at[i, ys] if d == FAR else self.zr1f.at[d - 1, i, ys]
-                    self.z1[i][h][d] = cp.make(acc.at[zi, ys, 1, rows, :], dst, to)
+                    self.z1[i][h][d] = make(acc.at[zi, ys, 1, rows, :], dst, to)
 
     def drain(self):
-        for d in COLUMNS:
-            self.sib[d].wait_send()
-            for copy in self.y0[d]:
-                copy.wait_send()
-        for copy in self.y1:
-            copy.wait_send()
-        for i in range(2):
-            for d in range(1, FAR + 1):
-                self.z0[i][d].wait_send()
-                for h in range(2):
-                    self.z1[i][h][d].wait_send()
+        self.cp.sent(self.group, RULER)
 
     def collect(self, d):
         me = self.me
@@ -253,7 +259,7 @@
                     total = tile if total is None else total + tile
                 dst[zi, yi, b] = total
                 return 0
-            lax.fori_loop(0, NY * 2, body, 0, unroll=4)
+            lax.fori_loop(0, NY * 2, body, 0, unroll=8)
 
         tiles(1 - me.c, self.snd)
         self.sib[d].start()
@@ -281,8 +287,7 @@
         me = self.me
         for d in cols:
             j = COLUMNS.index(d)
-            for copy in self.y0[d]:
-                copy.wait_recv()
+            self.cp.arrived(self.y0_slot[d], NY - 1)
             add(self.acc.at[me.zz(d), me.y, 0], *[self.yr.at[j, k] for k in range(NY - 1)])
             if d == FAR:
                 for i in range(2):
@@ -330,8 +335,7 @@
 
     def y1last(self):
         me = self.me
-        for copy in self.y1:
-            copy.wait_recv()
+        self.cp.arrived(self.y1_slot, NY - 1)
         add(self.acc.at[me.z, me.y, 1], *[self.yr1.at[k] for k in range(NY - 1)])
 
 
@@ -358,53 +362,49 @@
 
 def tables_kernel(slot_ref, len_ref, seen, source, rows_ref, span_of):
     chip = lax.axis_index("rail") // NC
-    lane = lax.broadcasted_iota(jnp.int32, (1, LANES), 1) % SPAN
 
     def invert(i, _):
         span_of[slot_ref[i]] = i
         return 0
 
-    lax.fori_loop(0, NSLOT, invert, 0, unroll=8)
-
+    lax.fori_loop(0, NSLOT, invert, 0, unroll=16)
     for s in range(SLOTS):
         def clear(i, _):
             source[s * NSLOT + i] = s * WT
             return 0
 
-        lax.fori_loop(0, NSLOT, clear, 0, unroll=8)
+        lax.fori_loop(0, NSLOT, clear, 0, unroll=32)
+
+    row = lax.broadcasted_iota(jnp.int32, (8, LANES), 0)
+    span_rows_ = jnp.zeros((8, LANES), jnp.int32)
+    for s in range(SLOTS):
         span = span_of[chip * SLOTS + s]
+        span_rows_ = jnp.where(row == s, span, span_rows_)
         seen[s * WT] = 0
-
-        def fill(w, _):
+        for w in range(1, WT):
             n = span - (WT - 1) + w
             j = slot_ref[jnp.maximum(n, 0)]
-            j = (j // 16) * 16 + (j % 4) * 4 + (j // 4) % 4
+            j = (j & ~15) | ((j & 3) << 2) | ((j >> 2) & 3)
             seen[s * WT + w] = j
-
-            @pl.when(n >= 0)
-            def _():
-                source[s * NSLOT + j] = s * WT + w
-
-            return 0
-
-        lax.fori_loop(1, WT, fill, 0)
-        qpos = span * SPAN + lane
-        qstart = jnp.zeros((1, LANES), jnp.int32)
-        end = 0
-        for i in range(len_ref.shape[0]):
-            end = end + len_ref[i]
-            qstart = jnp.where(qpos >= end, end, qstart)
-        rows_ref[s, 0:1, :] = qstart - (span - (WT - 1)) * SPAN
-        rows_ref[s, 1:2, :] = qpos - qstart
+            source[jnp.where(n >= 0, s * NSLOT + j, SLOTS * NSLOT)] = s * WT + w
+    lane = lax.broadcasted_iota(jnp.int32, (8, LANES), 1) % SPAN
+    qpos = span_rows_ * SPAN + lane
+    qstart = jnp.zeros((8, LANES), jnp.int32)
+    end = 0
+    for i in range(len_ref.shape[0]):
+        end = end + len_ref[i]
+        qstart = jnp.where(qpos >= end, end, qstart)
+    rows_ref[0] = qstart - (span_rows_ - (WT - 1)) * SPAN
+    rows_ref[1] = qpos - qstart
 
 
 def kernel(seen, source, rows_ref, q_ref, o_ref, k_ref, v_ref, dq_ref, dk_ref, dv_ref,
-           k_all, v_all, qm, om, kw, vw, qs, os_, tq, s_scr, p_scr, wk, wv, inv_scr, dqt, dqm,
+           k_all, v_all, qm, om, kw, vw, qs, os_, tq, s_scr, p_scr, wk, wv, inv_scr, dqm,
            *rest):
     bufs_v, bufs_k = rest[:9], rest[9:18]
     send, recv, local = rest[18:]
     me = Place()
-    cp = Copies(send, recv)
+    cp = Copies(send, recv, k_all)
     x, z, y, c = me.x, me.z, me.y, me.c
     j_me = x * NC + c
 
@@ -414,77 +414,86 @@
     kvx = [[], []]
     own = []
     mine = pl.ds(pl.multiple_of((x % 2) * ROWS, ROWS), ROWS)
+    kvx_slot = [cp.slot(), cp.slot()]
     for i, (src, dst) in enumerate(((k_ref, k_all), (v_ref, v_all))):
         for step in range(1, NX):
             to = (x + step) % NX
             kvx[i].append(cp.make(
-                src.at[:, cols(to, HEAD)], dst.at[line(z, c, x // 2) + y, mine, :], me.at(x=to)))
+                src.at[:, cols(to, HEAD)], dst.at[line(z, c, x // 2) + y, mine, :], me.at(x=to),
+                0, kvx_slot[i]))
         own.append(pltpu.make_async_copy(
             src.at[:, cols(x, HEAD)], dst.at[line(z, c, x // 2) + y, mine, :], local.at[i]))
     rows = pl.ds(pl.multiple_of(c * BLOCK + x * ROWS, ROWS), ROWS)
-    qo = []
-    for j, dev in me.team():
-        for src, dst in ((q_ref, qm), (o_ref, om)):
-            qo.append(cp.make(src.at[:, cols(j, WIDE)], dst.at[rows, :], dev))
+    qo = [[], []]
+    qo_slot = [cp.slot(), cp.slot()]
     for i, (src, dst) in enumerate(((q_ref, qm), (o_ref, om))):
+        for j, dev in me.team():
+            qo[i].append(cp.make(
+                src.at[:, cols(j, WIDE)], dst.at[rows, :], dev, 0, qo_slot[i]))
         own.append(pltpu.make_async_copy(
             src.at[:, cols(j_me, WIDE)], dst.at[rows, :], local.at[2 + i]))
-    gk, gv = Gather(me, cp, k_all), Gather(me, cp, v_all)
-    sv = Scatter(me, cp, wv, source, bufs_v)
-    sk = Scatter(me, cp, wk, source, bufs_k)
+    gk, gv = Gather(me, cp, k_all, 1), Gather(me, cp, v_all, 2)
+    sv = Scatter(me, cp, wv, source, bufs_v, 3)
+    sk = Scatter(me, cp, wk, source, bufs_k, 4)
     dqs = []
+    dqs_slot = cp.slot()
     for j, dev in me.team():
         there = pl.ds(pl.multiple_of((j % NC) * BLOCK + (j // NC) * ROWS, ROWS), ROWS)
-        dqs.append(cp.make(dqm.at[there, :], dq_ref.at[:, cols(j_me, WIDE)], dev))
+        dqs.append(cp.make(
+            dqm.at[there, :], dq_ref.at[:, cols(j_me, WIDE)], dev, 0, dqs_slot))
     own.append(pltpu.make_async_copy(dqm.at[rows, :], dq_ref.at[:, cols(j_me, WIDE)], local.at[4]))
     back = [[], []]
+    back_slot = [cp.slot(), cp.slot()]
     for i, (acc, dst) in enumerate(((bufs_k[0], dk_ref), (bufs_v[0], dv_ref))):
         for step in range(1, NX):
             to = (x + step) % NX
             part = pl.ds(pl.multiple_of((to % 2) * ROWS, ROWS), ROWS)
             back[i].append(cp.make(
-                acc.at[z, y, to // 2, part, :], dst.at[:, cols(x, HEAD)], me.at(x=to)))
+                acc.at[z, y, to // 2, part, :], dst.at[:, cols(x, HEAD)], me.at(x=to),
+                0, back_slot[i]))
         own.append(pltpu.make_async_copy(
             acc.at[z, y, x // 2, mine, :], dst.at[:, cols(x, HEAD)], local.at[5 + i]))
-    assert cp.count <= N_SEM
+    assert cp.count <= N_RECV
 
     greet(me)
     for i in range(2):
         for copy in kvx[i]:
             copy.start()
         own[i].start()
-    for copy in qo:
-        copy.start()
-    own[2].start()
-    own[3].start()
-
-    for copy in kvx[0]:
-        copy.wait_recv()
+    cp.arrived(kvx_slot[0], NX - 1, ROWS)
     own[0].wait()
     gk.begin()
+    for i in range(2):
+        for copy in qo[i]:
+            copy.start()
+        own[2 + i].start()
+    gk.near(1)
     gk.second()
-    for copy in kvx[1]:
-        copy.wait_recv()
+    gk.finish(0)
+    gk.near(2)
+    gk.wide(1)
+    gk.finish(1, -1)
+    cp.arrived(kvx_slot[1], NX - 1, ROWS)
     own[1].wait()
     gv.begin()
-    gk.zstep(1)
-    gk.finish(0)
+    gk.near(3)
+    gk.wide(2)
+    gk.finish(2, -2)
+    gv.near(1)
     gv.second()
-    gk.zstep(2)
-    gk.finish(1, -1)
-    gk.zstep(3)
-    gv.zstep(1)
-    gk.finish(2, -2)
-    gk.zstep(4)
+    gk.near(4)
+    gk.wide(3)
+    gv.near(2)
+    gv.finish(0)
     gk.finish(3, -3)
-    gv.finish(0)
-    gv.zstep(2)
     gk.finish(4)
+    gv.wide(1)
+    gv.finish(1, -1)
+    gk.wide(4)
     gk.done()
-    for copy in qo:
-        copy.wait_recv()
-    own[2].wait()
-    own[3].wait()
+    for i in range(2):
+        cp.arrived(qo_slot[i], 14)
+        own[2 + i].wait()
 
     sub = lax.broadcasted_iota(jnp.int32, (STEP, 1), 0)
 
@@ -497,7 +506,7 @@
                         event()
 
     def first_part(s, _):
-        low, extra = rows_ref[s, 0:1, :], rows_ref[s, 1:2, :]
+        low, extra = rows_ref[0, pl.ds(s, 1), :], rows_ref[1, pl.ds(s, 1), :]
 
         def put(w, tile):
             kw[s, span_rows(w), :] = tile
@@ -536,18 +545,18 @@
         return 0
 
     v_events = [
-        [[lambda: gv.finish(1, -1)], [lambda: gv.zstep(4)], [lambda: gv.finish(3, -3)], None],
-        [None, None, None, None],
-        [[lambda: gv.zstep(3)], [lambda: gv.finish(2, -2)], [lambda: gv.finish(4)], None],
+        [[lambda: gv.near(3)], [lambda: gv.near(4)], [lambda: gv.finish(4)], None],
+        [[lambda: gv.wide(2)], [lambda: gv.wide(3)], [lambda: gv.wide(4)], None],
+        [[lambda: gv.finish(2, -2)], [lambda: gv.finish(3, -3)], None, None],
     ]
     lax.fori_loop(0, SLOTS, first_part, 0)
     gv.done()
 
     sv.collect(4)
     sv.collect(3)
+    sv.pair(4)
     sv.collect(-3)
-    sv.pair(4)
-    sv.pair(3, -3)
+    sv.pair(3)
 
     def second_part(s, _):
 
@@ -564,87 +573,97 @@
             total = total + fold(p_scr[s, t].astype(F32) * dp, jnp.sum)
         during(s, k_events[0])
         dots = jnp.sum(total, axis=0, keepdims=True) * inv_scr[s, :1, :]
-        dqt[...] = jnp.zeros_like(dqt)
         for t in range(STEPS):
             ds = (p_scr[s, t].astype(F32) * (s_scr[t] - dots)).astype(BF16)
+            p_scr[s, t] = ds
             dk = jnp.dot(ds, qs[s], preferred_element_type=F32) * SCALE
             wk[pl.ds(s * WT + 2 * t, 2)] = dk.astype(BF16).reshape(2, SPAN, HEAD)
-            dqt[...] += lax.dot_general(kw[s, at_step(t), :], ds, (((0,), (0,)), ((), ())),
-                                        preferred_element_type=F32)
+        during(s, k_events[1])
+        return 0
+
+    def third_part(s, _):
+        total = jnp.zeros((HEAD, LANES), F32)
+        for t in range(STEPS):
+            total = total + lax.dot_general(kw[s, at_step(t), :], p_scr[s, t],
+                                            (((0,), (0,)), ((), ())), preferred_element_type=F32)
         for h in range(QHEADS):
             dqm[span_rows(s), h * HEAD:(h + 1) * HEAD] = (
-                (dqt[:, h * SPAN:(h + 1) * SPAN] * SCALE).T.astype(BF16))
-        during(s, k_events[1])
+                (total[:, h * SPAN:(h + 1) * SPAN] * SCALE).T.astype(BF16))
+        during(s, q_events)
         return 0
 
     k_events = [
         [
-            [lambda: sv.collect(2), lambda: sv.collect(-2)],
-            [lambda: sv.collect(1), lambda: sv.collect(-1), lambda: sv.z1step(2)],
-            [lambda: sv.collect(0), lambda: sv.pair(1, -1)],
+            [lambda: sv.collect(2), lambda: sv.pair(-3), lambda: sv.collect(-2)],
+            [lambda: sv.yadd(4), lambda: sv.collect(1), lambda: sv.collect(-1)],
+            [lambda: sv.z1step(2), lambda: sv.pair(1, -1)],
             [lambda: sv.z0step(2), lambda: sv.z1step(1)],
         ],
         [
-            [lambda: sv.z1step(3), lambda: sv.pair(2, -2), lambda: sv.yadd(4)],
-            [lambda: sv.yadd(3, -3), lambda: sv.z0step(3)],
+            [lambda: sv.z1step(3), lambda: sv.pair(2, -2)],
+            [lambda: sv.yadd(3, -3), lambda: sv.z0step(3), lambda: sv.collect(0)],
             [lambda: sv.yadd(2, -2), lambda: sv.pair(0)],
             [lambda: sv.yadd(1, -1)],
         ],
     ]
     lax.fori_loop(0, SLOTS, second_part, 0)
-    for copy in dqs:
-        copy.start()
-    own[4].start()
 
     sk.collect(4)
+    sk.collect(3)
     sv.z0step(1)
-    sk.collect(3)
+    sk.pair(4)
     sk.collect(-3)
-    sk.pair(4)
     sv.z1last()
+    sk.pair(3)
     sk.collect(2)
+    sk.pair(-3)
     sk.collect(-2)
-    sk.pair(3, -3)
+    sk.z1step(3)
+    sk.pair(2, -2)
     sv.yadd(0)
+    sv.z0last()
     sk.yadd(4)
     sk.collect(1)
     sk.collect(-1)
-    sk.z1step(3)
-    sk.pair(2, -2)
-    sv.z0last()
-    sk.yadd(3, -3)
-    sk.z0step(3)
-    sk.collect(0)
     sv.y1last()
     for copy in back[1]:
         copy.start()
     own[6].start()
-    sk.pair(1, -1)
-    sk.pair(0)
-    sk.z1step(2)
-    sk.yadd(2, -2)
-    sk.z0step(2)
-    sk.yadd(1, -1)
-    gk.drain()
-    sk.z1step(1)
+    sk.yadd(3, -3)
+    q_events = [
+        [lambda: sk.z0step(3), lambda: sk.z1step(2), lambda: sk.pair(1, -1)],
+        [lambda: sk.collect(0), lambda: sk.yadd(2, -2)],
+        [lambda: sk.z0step(2), lambda: sk.pair(0)],
+        [lambda: sk.z1step(1), lambda: sk.yadd(1, -1)],
+    ]
+    lax.fori_loop(0, SLOTS, third_part, 0)
+    for copy in dqs:
+        copy.start()
+    own[4].start()
     sk.z0step(1)
     sk.yadd(0)
+    sk.z1last()
+    gk.drain()
     gv.drain()
-    sk.z1last()
-    for copy in kvx[0] + kvx[1] + qo:
-        copy.wait_send()
+    sv.drain()
     sk.z0last()
-    sv.drain()
     sk.y1last()
     for copy in back[0]:
         copy.start()
     own[5].start()
     sk.drain()
-    for copy in dqs + back[1] + back[0]:
-        copy.wait_recv()
-        copy.wait_send()
+    cp.arrived(dqs_slot, 14)
+    for i in range(2):
+        cp.arrived(back_slot[i], NX - 1, ROWS)
+    cp.sent(0, 48)
     for i in (4, 5, 6):
         own[i].wait()
+
+
+def settle_kernel(dq_in, dk_in, dv_in, dq_out, dk_out, dv_out):
+    dq_out[...] = dq_in[...]
+    dk_out[...] = dk_in[...]
+    dv_out[...] = dv_in[...]
 
 
 def per_device(queries, keys, values, output_cotangent, doc_lengths, span_slot):
@@ -669,8 +688,8 @@
         tables_kernel,
         out_shape=[
             jax.ShapeDtypeStruct((SLOTS * WT,), jnp.int32),
-            jax.ShapeDtypeStruct((SLOTS * NSLOT,), jnp.int32),
-            jax.ShapeDtypeStruct((SLOTS, 8, LANES), jnp.int32),
+            jax.ShapeDtypeStruct((SLOTS * NSLOT + 8,), jnp.int32),
+            jax.ShapeDtypeStruct((2, 8, LANES), jnp.int32),
         ],
         in_specs=[smem] * 2,
         out_specs=[smem, smem, pl.BlockSpec(memory_space=pltpu.VMEM)],
@@ -701,17 +720,23 @@
             vmem(SLOTS * WT, SPAN, HEAD),
             vmem(SLOTS * WT, SPAN, HEAD),
             vmem(SLOTS, 8, LANES, dtype=F32),
-            vmem(HEAD, LANES, dtype=F32),
             vmem(SLOTS * SPAN, WIDE),
         ] + scatter_bufs * 2 + [
-            pltpu.SemaphoreType.DMA((N_SEM,)),
-            pltpu.SemaphoreType.DMA((N_SEM,)),
+            pltpu.SemaphoreType.DMA((N_SEND,)),
+            pltpu.SemaphoreType.DMA((N_RECV,)),
             pltpu.SemaphoreType.DMA((8,)),
         ],
         compiler_params=pltpu.CompilerParams(
             collective_id=0, has_side_effects=True, vmem_limit_bytes=60 * 1024 * 1024),
         name="attention_backward",
     )(seen, source, rows, queries, output_cotangent, keys, values)
+    outs = pl.pallas_call(
+        settle_kernel,
+        out_shape=[jax.ShapeDtypeStruct(out.shape, out.dtype) for out in outs],
+        in_specs=[pl.BlockSpec(memory_space=pltpu.VMEM)] * 3,
+        out_specs=[pl.BlockSpec(memory_space=pltpu.VMEM)] * 3,
+        name="settle",
+    )(*outs)
     return tuple(outs)
 
 

time: 117 us -> 104 us (0.89)
  Pallas kernels: 112 us -> 103 us
  local copies, waits for them, and re-layouts: 3.4 us -> 0 us
    pallas_call x1, Pallas kernels: 108 us -> 99.2 us  [per_device(): pl.pallas_call(kernel, out_shape=[jax.ShapeDtypeStruct(queries.shape, BF1...]
    unnamed x7 -> x0, local copies, waits for them, and re-layouts: 3.4 us -> none
    pallas_call x0 -> x1, Pallas kernels: none -> 1.92 us  [per_device(): pl.pallas_call(settle_kernel, out_shape=[jax.ShapeDtypeStruct(out.shape,...]
    pallas_call x1, Pallas kernels: 3.86 us -> 2.23 us  [per_device(): pl.pallas_call(tables_kernel, out_shape=[jax.ShapeDtypeStruct((SLOTS * WT...]
where the time goes in v3:
time: 104 us
  Pallas kernels  103 us (99%)
    pallas_call x1, Pallas kernels, per_device(): pl.pallas_call(kernel, out_shape=[jax.ShapeDtypeStruct(queries.shape, BF1...  99.2 us
    pallas_call x1, Pallas kernels, per_device(): pl.pallas_call(tables_kernel, out_shape=[jax.ShapeDtypeStruct((SLOTS * WT...  2.23 us

profile of v3, /device:TPU:2, one launch (start us, length us, event | category | flops | bytes accessed | tf_op | source)
XLA Modules:
  0.0 104.0 jit_solution(12675626677510931491)
XLA Ops:
  0.6 2.2 %tables.1 = (s32[72]{0:T(128)}, s32[520]{0:T(1024)}, s32[2,8,512]{2,1,0:T(8,128)}) custom-call(s32[128]{0:T(128)} %slot_ref.1, s32[16]{0:T(128)} %len_ref.1), custom_call_target="tpu_custom_call" | custom-call | tf_op jit(solution)/shard_map/tables/pallas_call | solution.py:687
  2.9 99.2 %attention_backward.1 = (bf16[64,4096]{1,0:T(8,128)(2,1)}, bf16[64,512]{1,0:T(8,128)(2,1)}, bf16[64,512]{1,0:T(8,128)(2,1)}) custom-call(s32[72]{0:T(128)} %get-tuple-element.9.seen, s32[520]{0:T(1024)} %get-tuple-element.10.source, s32[2,8,512]{2,1,0:T(8,128)} %get-tuple-element.11.rows_ref, bf16[64,4096]{1,0:T(8,128)(2,1)} %q_ref.1, ...), custom_call_target="tpu_custom_call" | custom-call | tf_op jit(solution)/shard_map/attention_backward/pallas_call | solution.py:699
  102.0 1.9 %settle.1 = (bf16[64,4096]{1,0:T(8,128)(2,1)}, bf16[64,512]{1,0:T(8,128)(2,1)}, bf16[64,512]{1,0:T(8,128)(2,1)}) custom-call(bf16[64,4096]{1,0:T(8,128)(2,1)} %get-tuple-element.12.dq_in, bf16[64,512]{1,0:T(8,128)(2,1)} %get-tuple-element.13.dk_in, bf16[64,512]{1,0:T(8,128)(2,1)} %get-tuple-element.14.dv_in), custom_call_target="tpu_custom_call" | custom-call | tf_op jit(solution)/shard_map/settle/pallas_call | solution.py:733

commit v4 on v3

--- a/solution.py
+++ b/solution.py
@@ -17,10 +17,7 @@
 QHEADS = 4
 LANES = QHEADS * SPAN
 WIDE = QHEADS * HEAD
-STEP = 256
-STEPS = 9
-WIN = STEP * STEPS
-WT = WIN // SPAN
+WT = 17
 HALF = SPAN // 2
 FAR = NZ // 2
 SCALE = 1.0 / math.sqrt(HEAD)
@@ -174,15 +171,16 @@
             for copy in self.y[FAR]:
                 copy.start()
 
-    def wide(self, d):
-        for k in (0, 3, 2, 1):
+    def wide(self, d, half):
+        for k in ((0, 3), (2, 1))[half]:
             for i in range(2):
                 self.z2[i][k][d].wait_recv()
                 if d < FAR:
                     self.z2[i][k][d + 1].start()
-        self.sib[1][d].start()
-        if d < FAR:
-            self.sib[1][-d].start()
+        if half:
+            self.sib[1][d].start()
+            if d < FAR:
+                self.sib[1][-d].start()
 
     def finish(self, *cols):
         for d in cols:
@@ -197,6 +195,9 @@
 
 
 def add(dst, *srcs):
+    if len(srcs) == 1:
+        dst[...] += srcs[0][...]
+        return
     total = dst[...].astype(F32)
     for src in srcs:
         total = total + src[...].astype(F32)
@@ -271,11 +272,7 @@
             zi = me.zz(d)
             self.sib[d].wait_recv()
 
-            def body(yi, _):
-                add(self.acc.at[zi, yi], self.sibr.at[zi, yi])
-                return 0
-
-            lax.fori_loop(0, NY, body, 0)
+            add(self.acc.at[zi], self.sibr.at[zi])
             for copy in self.y0[d]:
                 copy.start()
             if d == FAR:
@@ -304,18 +301,17 @@
                 add(self.acc.at[zi, me.y, 0], self.zr0f.at[d, i])
             self.z0[i][d].start()
 
-    def z1step(self, d):
+    def z1step(self, d, h):
         me = self.me
-        for h in range(2):
-            for i, sign in enumerate((1, -1)):
-                self.z1[i][h][d + 1].wait_recv()
-                zi = me.zz(sign * d)
-                for yi in range(2 * h, 2 * h + 2):
-                    if d == FAR - 1:
-                        add(self.acc.at[zi, yi, 1, pl.ds(i * HALF, HALF), :], self.zr1h.at[i, yi])
-                    else:
-                        add(self.acc.at[zi, yi, 1], self.zr1f.at[d, i, yi])
-                self.z1[i][h][d].start()
+        for i, sign in enumerate((1, -1)):
+            self.z1[i][h][d + 1].wait_recv()
+            zi = me.zz(sign * d)
+            for yi in range(2 * h, 2 * h + 2):
+                if d == FAR - 1:
+                    add(self.acc.at[zi, yi, 1, pl.ds(i * HALF, HALF), :], self.zr1h.at[i, yi])
+                else:
+                    add(self.acc.at[zi, yi, 1], self.zr1f.at[d, i, yi])
+            self.z1[i][h][d].start()
 
     def z1last(self):
         me = self.me
@@ -343,21 +339,8 @@
     return op(x.reshape(x.shape[0] // 8, 8, x.shape[1]), axis=0)
 
 
-def at_step(t):
-    return pl.ds(t * STEP, STEP)
-
-
 def span_rows(i):
     return pl.ds(pl.multiple_of(i * SPAN, SPAN), SPAN)
-
-
-def load_window(s, seen, src, put):
-    def body(w, _):
-        j = seen[s * WT + w]
-        put(w, src[j])
-        return 0
-
-    lax.fori_loop(0, WT, body, 0, unroll=2)
 
 
 def tables_kernel(slot_ref, len_ref, seen, source, rows_ref, span_of):
@@ -370,7 +353,7 @@
     lax.fori_loop(0, NSLOT, invert, 0, unroll=16)
     for s in range(SLOTS):
         def clear(i, _):
-            source[s * NSLOT + i] = s * WT
+            source[s * NSLOT + i] = SLOTS * WT
             return 0
 
         lax.fori_loop(0, NSLOT, clear, 0, unroll=32)
@@ -380,8 +363,7 @@
     for s in range(SLOTS):
         span = span_of[chip * SLOTS + s]
         span_rows_ = jnp.where(row == s, span, span_rows_)
-        seen[s * WT] = 0
-        for w in range(1, WT):
+        for w in range(WT):
             n = span - (WT - 1) + w
             j = slot_ref[jnp.maximum(n, 0)]
             j = (j & ~15) | ((j & 3) << 2) | ((j >> 2) & 3)
@@ -399,7 +381,7 @@
 
 
 def kernel(seen, source, rows_ref, q_ref, o_ref, k_ref, v_ref, dq_ref, dk_ref, dv_ref,
-           k_all, v_all, qm, om, kw, vw, qs, os_, tq, s_scr, p_scr, wk, wv, inv_scr, dqm,
+           k_all, v_all, qm, om, qs, os_, ot, tq, s_scr, p_scr, wk, wv, inv_scr, dqm,
            *rest):
     bufs_v, bufs_k = rest[:9], rest[9:18]
     send, recv, local = rest[18:]
@@ -471,31 +453,46 @@
     gk.second()
     gk.finish(0)
     gk.near(2)
-    gk.wide(1)
-    gk.finish(1, -1)
+    gk.finish(-1)
+    gk.wide(1, 0)
+    gk.finish(1)
+    gk.wide(1, 1)
     cp.arrived(kvx_slot[1], NX - 1, ROWS)
     own[1].wait()
     gv.begin()
     gk.near(3)
-    gk.wide(2)
-    gk.finish(2, -2)
+    gk.finish(-2)
+    gk.wide(2, 0)
+    gk.finish(2)
+    gk.wide(2, 1)
     gv.near(1)
     gv.second()
     gk.near(4)
-    gk.wide(3)
+    gv.finish(0)
+    gk.wide(3, 0)
+    gk.finish(-3)
+    gk.wide(3, 1)
+    gk.finish(3)
     gv.near(2)
-    gv.finish(0)
-    gk.finish(3, -3)
+    gv.wide(1, 0)
+    gv.finish(-1)
+    gv.wide(1, 1)
+    gv.finish(1)
+    gk.wide(4, 0)
+    gk.wide(4, 1)
     gk.finish(4)
-    gv.wide(1)
-    gv.finish(1, -1)
-    gk.wide(4)
+    gv.near(3)
+    gv.finish(-2)
+    gv.wide(2, 0)
     gk.done()
     for i in range(2):
         cp.arrived(qo_slot[i], 14)
         own[2 + i].wait()
 
-    sub = lax.broadcasted_iota(jnp.int32, (STEP, 1), 0)
+    sub = lax.broadcasted_iota(jnp.int32, (SPAN, 1), 0)
+    wk[SLOTS * WT] = jnp.zeros((SPAN, HEAD), BF16)
+    wv[SLOTS * WT] = jnp.zeros((SPAN, HEAD), BF16)
+    mid = WT // 2
 
     def during(s, table):
         for i, events in enumerate(table):
@@ -505,28 +502,33 @@
                     for event in events:
                         event()
 
+    def dv_tile(s, t):
+        dv = jnp.dot(p_scr[s, t], os_[s], preferred_element_type=F32)
+        wv[s * WT + t] = dv.astype(BF16)
+
     def first_part(s, _):
         low, extra = rows_ref[0, pl.ds(s, 1), :], rows_ref[1, pl.ds(s, 1), :]
-
-        def put(w, tile):
-            kw[s, span_rows(w), :] = tile
-
-        load_window(s, seen, k_all, put)
+        before = jnp.maximum(s - 1, 0)
         for h in range(QHEADS):
             qh = qm[span_rows(s), h * HEAD:(h + 1) * HEAD]
             qs[s, h * SPAN:(h + 1) * SPAN, :] = qh
             tq[:, h * SPAN:(h + 1) * SPAN] = qh.T
         top = jnp.full((8, LANES), NEG, F32)
-        for t in range(STEPS):
-            st = jnp.dot(kw[s, at_step(t), :], tq[...], preferred_element_type=F32)
-            rel = (sub + t * STEP) - low
+        for t in range(WT):
+            if t == mid:
+                during(s, v_events[0])
+            st = jnp.dot(k_all[seen[s * WT + t]], tq[...], preferred_element_type=F32)
+            rel = (sub + t * SPAN) - low
             st = jnp.where((rel >= 0) & (rel <= extra), st, NEG)
             s_scr[t] = st
             top = jnp.maximum(top, fold(st, jnp.max))
-        during(s, v_events[0])
+        during(s, v_events[1])
         mc = jnp.max(top, axis=0, keepdims=True) * C2
         total = jnp.zeros((8, LANES), F32)
-        for t in range(STEPS):
+        for t in range(WT):
+            if t == mid:
+                during(s, v_events[2])
+            dv_tile(before, t)
             p = jnp.exp2(s_scr[t] * C2 - mc)
             p_scr[s, t] = p.astype(BF16)
             total = total + fold(p, jnp.sum)
@@ -536,55 +538,78 @@
         for h in range(QHEADS):
             col = inv8[:, h * SPAN:(h + 1) * SPAN].T[:, :1]
             oh = om[span_rows(s), h * HEAD:(h + 1) * HEAD].astype(F32)
-            os_[s, h * SPAN:(h + 1) * SPAN, :] = (oh * col).astype(BF16)
-        during(s, v_events[1])
-        for t in range(STEPS):
-            dv = jnp.dot(p_scr[s, t], os_[s], preferred_element_type=F32)
-            wv[pl.ds(s * WT + 2 * t, 2)] = dv.astype(BF16).reshape(2, SPAN, HEAD)
-        during(s, v_events[2])
+            oh = (oh * col).astype(BF16)
+            os_[s, h * SPAN:(h + 1) * SPAN, :] = oh
+            ot[s, :, h * SPAN:(h + 1) * SPAN] = oh.T
+        during(s, v_events[3])
         return 0
 
     v_events = [
-        [[lambda: gv.near(3)], [lambda: gv.near(4)], [lambda: gv.finish(4)], None],
-        [[lambda: gv.wide(2)], [lambda: gv.wide(3)], [lambda: gv.wide(4)], None],
-        [[lambda: gv.finish(2, -2)], [lambda: gv.finish(3, -3)], None, None],
+        [
+            [lambda: gv.finish(2)],
+            [lambda: gv.wide(3, 0), lambda: gv.finish(3)],
+            [lambda: gv.wide(3, 1)],
+            [lambda: gv.wide(4, 0)],
+        ],
+        [
+            [lambda: gv.wide(2, 1)],
+            None,
+            [lambda: gv.finish(4)],
+            None,
+        ],
+        [
+            [lambda: gv.near(4)],
+            None,
+            None,
+            None,
+        ],
+        [
+            [lambda: gv.finish(-3)],
+            None,
+            None,
+            [lambda: gv.wide(4, 1)],
+        ],
     ]
     lax.fori_loop(0, SLOTS, first_part, 0)
-    gv.done()
+    for t in range(WT):
+        dv_tile(SLOTS - 1, t)
 
     sv.collect(4)
     sv.collect(3)
+    sv.collect(-3)
+    gv.done()
+    sv.collect(2)
+    sv.collect(-2)
+    sv.collect(1)
     sv.pair(4)
-    sv.collect(-3)
+    sv.collect(-1)
+    sv.collect(0)
     sv.pair(3)
 
     def second_part(s, _):
-
-        def put(w, tile):
-            vw[span_rows(w), :] = tile
-
-        load_window(s, seen, v_all, put)
-        for h in range(QHEADS):
-            tq[:, h * SPAN:(h + 1) * SPAN] = os_[s, h * SPAN:(h + 1) * SPAN, :].T
         total = jnp.zeros((8, LANES), F32)
-        for t in range(STEPS):
-            dp = jnp.dot(vw[at_step(t), :], tq[...], preferred_element_type=F32)
+        for t in range(WT):
+            if t == mid:
+                during(s, k_events[0])
+            dp = jnp.dot(v_all[seen[s * WT + t]], ot[s], preferred_element_type=F32)
             s_scr[t] = dp
             total = total + fold(p_scr[s, t].astype(F32) * dp, jnp.sum)
-        during(s, k_events[0])
+        during(s, k_events[1])
         dots = jnp.sum(total, axis=0, keepdims=True) * inv_scr[s, :1, :]
-        for t in range(STEPS):
+        for t in range(WT):
+            if t == mid:
+                during(s, k_events[2])
             ds = (p_scr[s, t].astype(F32) * (s_scr[t] - dots)).astype(BF16)
             p_scr[s, t] = ds
             dk = jnp.dot(ds, qs[s], preferred_element_type=F32) * SCALE
-            wk[pl.ds(s * WT + 2 * t, 2)] = dk.astype(BF16).reshape(2, SPAN, HEAD)
-        during(s, k_events[1])
+            wk[s * WT + t] = dk.astype(BF16)
+        during(s, k_events[3])
         return 0
 
     def third_part(s, _):
         total = jnp.zeros((HEAD, LANES), F32)
-        for t in range(STEPS):
-            total = total + lax.dot_general(kw[s, at_step(t), :], p_scr[s, t],
+        for t in range(WT):
+            total = total + lax.dot_general(k_all[seen[s * WT + t]], p_scr[s, t],
                                             (((0,), (0,)), ((), ())), preferred_element_type=F32)
         for h in range(QHEADS):
             dqm[span_rows(s), h * HEAD:(h + 1) * HEAD] = (
@@ -594,57 +619,80 @@
 
     k_events = [
         [
-            [lambda: sv.collect(2), lambda: sv.pair(-3), lambda: sv.collect(-2)],
-            [lambda: sv.yadd(4), lambda: sv.collect(1), lambda: sv.collect(-1)],
-            [lambda: sv.z1step(2), lambda: sv.pair(1, -1)],
-            [lambda: sv.z0step(2), lambda: sv.z1step(1)],
+            [lambda: sv.pair(-3)],
+            [lambda: sv.pair(1)],
+            None,
+            [lambda: sv.yadd(-2)],
         ],
         [
-            [lambda: sv.z1step(3), lambda: sv.pair(2, -2)],
-            [lambda: sv.yadd(3, -3), lambda: sv.z0step(3), lambda: sv.collect(0)],
-            [lambda: sv.yadd(2, -2), lambda: sv.pair(0)],
-            [lambda: sv.yadd(1, -1)],
+            None,
+            [lambda: sv.yadd(3)],
+            [lambda: sv.z1step(2, 1), lambda: sv.z0step(3), lambda: sv.yadd(2)],
+            None,
+        ],
+        [
+            [lambda: sv.z1step(3, 0), lambda: sv.pair(2)],
+            [lambda: sv.pair(-1)],
+            None,
+            [lambda: sv.z1step(1, 0)],
+        ],
+        [
+            [lambda: sv.z1step(3, 1), lambda: sv.pair(-2), lambda: sv.yadd(4)],
+            [lambda: sv.z1step(2, 0), lambda: sv.yadd(-3), lambda: sv.pair(0)],
+            None,
+            None,
         ],
     ]
     lax.fori_loop(0, SLOTS, second_part, 0)
 
     sk.collect(4)
     sk.collect(3)
-    sv.z0step(1)
+    sk.collect(-3)
+    sk.collect(2)
+    sk.collect(-2)
+    sk.collect(1)
     sk.pair(4)
-    sk.collect(-3)
-    sv.z1last()
+    sk.collect(-1)
+    sk.collect(0)
     sk.pair(3)
-    sk.collect(2)
+    sv.z0step(2)
+    sv.z1step(1, 1)
+    sv.yadd(1)
     sk.pair(-3)
-    sk.collect(-2)
-    sk.z1step(3)
-    sk.pair(2, -2)
+    sv.yadd(-1)
     sv.yadd(0)
-    sv.z0last()
-    sk.yadd(4)
-    sk.collect(1)
-    sk.collect(-1)
-    sv.y1last()
-    for copy in back[1]:
-        copy.start()
-    own[6].start()
-    sk.yadd(3, -3)
     q_events = [
-        [lambda: sk.z0step(3), lambda: sk.z1step(2), lambda: sk.pair(1, -1)],
-        [lambda: sk.collect(0), lambda: sk.yadd(2, -2)],
-        [lambda: sk.z0step(2), lambda: sk.pair(0)],
-        [lambda: sk.z1step(1), lambda: sk.yadd(1, -1)],
+        [lambda: sk.z1step(3, 0), lambda: sk.pair(2), lambda: sk.z1step(3, 1)],
+        [lambda: sk.yadd(4), lambda: sk.pair(-2), lambda: sk.pair(1), lambda: sv.z0step(1)],
+        [lambda: sk.yadd(3), lambda: sk.pair(-1), lambda: sv.z1last()],
+        None,
     ]
     lax.fori_loop(0, SLOTS, third_part, 0)
     for copy in dqs:
         copy.start()
     own[4].start()
+    sk.z1step(2, 0)
+    sk.yadd(-3)
+    sk.pair(0)
+    sk.yadd(2)
+    sk.z1step(2, 1)
+    sk.z0step(3)
+    sv.z0last()
+    sk.yadd(-2)
+    gk.drain()
+    sk.yadd(1)
+    sk.z1step(1, 0)
+    sk.yadd(-1)
+    sk.z1step(1, 1)
+    sk.z0step(2)
+    sv.y1last()
+    for copy in back[1]:
+        copy.start()
+    own[6].start()
+    sk.yadd(0)
+    gv.drain()
+    sk.z1last()
     sk.z0step(1)
-    sk.yadd(0)
-    sk.z1last()
-    gk.drain()
-    gv.drain()
     sv.drain()
     sk.z0last()
     sk.y1last()
@@ -710,15 +758,14 @@
             vmem(NSLOT, SPAN, HEAD),
             vmem(SLOTS * SPAN, WIDE),
             vmem(SLOTS * SPAN, WIDE),
-            vmem(SLOTS, WIN, HEAD),
-            vmem(WIN, HEAD),
             vmem(SLOTS, LANES, HEAD),
             vmem(SLOTS, LANES, HEAD),
+            vmem(SLOTS, HEAD, LANES),
             vmem(HEAD, LANES),
-            vmem(STEPS, STEP, LANES, dtype=F32),
-            vmem(SLOTS, STEPS, STEP, LANES),
-            vmem(SLOTS * WT, SPAN, HEAD),
-            vmem(SLOTS * WT, SPAN, HEAD),
+            vmem(WT, SPAN, LANES, dtype=F32),
+            vmem(SLOTS, WT, SPAN, LANES),
+            vmem(SLOTS * WT + 1, SPAN, HEAD),
+            vmem(SLOTS * WT + 1, SPAN, HEAD),
             vmem(SLOTS, 8, LANES, dtype=F32),
             vmem(SLOTS * SPAN, WIDE),
         ] + scatter_bufs * 2 + [

time: 104 us -> 98.5 us (0.947)
  Pallas kernels: 103 us -> 97.5 us
    pallas_call x1, Pallas kernels: 99.2 us -> 93.4 us  [per_device(): pl.pallas_call(kernel, out_shape=[jax.ShapeDtypeStruct(queries.shape, BF1...]
where the time goes in v4:
time: 98.5 us; the launch traced here: 98.2 us
  Pallas kernels  97.5 us (99%)
    pallas_call x1, Pallas kernels, per_device(): pl.pallas_call(kernel, out_shape=[jax.ShapeDtypeStruct(queries.shape, BF1...  93.4 us
    pallas_call x1, Pallas kernels, per_device(): pl.pallas_call(tables_kernel, out_shape=[jax.ShapeDtypeStruct((SLOTS * WT...  2.22 us

profile of v4, /device:TPU:2, one launch (start us, length us, event | category | flops | bytes accessed | tf_op | source)
XLA Modules:
  0.0 98.2 jit_solution(14734578231033942205)
XLA Ops:
  0.6 2.2 %tables.1 = (s32[68]{0:T(128)}, s32[520]{0:T(1024)}, s32[2,8,512]{2,1,0:T(8,128)}) custom-call(s32[128]{0:T(128)} %slot_ref.1, s32[16]{0:T(128)} %len_ref.1), custom_call_target="tpu_custom_call" | custom-call | tf_op jit(solution)/shard_map/tables/pallas_call | solution.py:735
  2.9 93.4 %attention_backward.1 = (bf16[64,4096]{1,0:T(8,128)(2,1)}, bf16[64,512]{1,0:T(8,128)(2,1)}, bf16[64,512]{1,0:T(8,128)(2,1)}) custom-call(s32[68]{0:T(128)} %get-tuple-element.9.seen, s32[520]{0:T(1024)} %get-tuple-element.10.source, s32[2,8,512]{2,1,0:T(8,128)} %get-tuple-element.11.rows_ref, bf16[64,4096]{1,0:T(8,128)(2,1)} %q_ref.1, ...), custom_call_target="tpu_custom_call" | custom-call | tf_op jit(solution)/shard_map/attention_backward/pallas_call | solution.py:747
  96.2 1.9 %settle.1 = (bf16[64,4096]{1,0:T(8,128)(2,1)}, bf16[64,512]{1,0:T(8,128)(2,1)}, bf16[64,512]{1,0:T(8,128)(2,1)}) custom-call(bf16[64,4096]{1,0:T(8,128)(2,1)} %get-tuple-element.12.dq_in, bf16[64,512]{1,0:T(8,128)(2,1)} %get-tuple-element.13.dk_in, bf16[64,512]{1,0:T(8,128)(2,1)} %get-tuple-element.14.dv_in), custom_call_target="tpu_custom_call" | custom-call | tf_op jit(solution)/shard_map/settle/pallas_call | solution.py:780

commit v5 on v4

--- a/solution.py
+++ b/solution.py
@@ -18,6 +18,7 @@
 LANES = QHEADS * SPAN
 WIDE = QHEADS * HEAD
 WT = 17
+PAD = WT + 2
 HALF = SPAN // 2
 FAR = NZ // 2
 SCALE = 1.0 / math.sqrt(HEAD)
@@ -343,45 +344,46 @@
     return pl.ds(pl.multiple_of(i * SPAN, SPAN), SPAN)
 
 
-def tables_kernel(slot_ref, len_ref, seen, source, rows_ref, span_of):
-    chip = lax.axis_index("rail") // NC
-
-    def invert(i, _):
-        span_of[slot_ref[i]] = i
-        return 0
-
-    lax.fori_loop(0, NSLOT, invert, 0, unroll=16)
+def swap_fields(j):
+    return (j & ~15) | ((j & 3) << 2) | ((j >> 2) & 3)
+
+
+def make_tables(chip, slot_ref, slot_row, len_ref, seen, source, rows_scr):
+    numbers = lax.broadcasted_iota(jnp.int32, (1, NSLOT), 1)
+    slots = slot_row[...]
+
+    def span_in(j):
+        return jnp.sum(jnp.where(slots == j, numbers, 0))
+
+    spans = [span_in(chip * SLOTS + s) for s in range(SLOTS)]
+    row = lax.broadcasted_iota(jnp.int32, (8, LANES), 0)
+    base = jnp.zeros((8, LANES), jnp.int32)
     for s in range(SLOTS):
-        def clear(i, _):
-            source[s * NSLOT + i] = SLOTS * WT
-            return 0
-
-        lax.fori_loop(0, NSLOT, clear, 0, unroll=32)
-
-    row = lax.broadcasted_iota(jnp.int32, (8, LANES), 0)
-    span_rows_ = jnp.zeros((8, LANES), jnp.int32)
-    for s in range(SLOTS):
-        span = span_of[chip * SLOTS + s]
-        span_rows_ = jnp.where(row == s, span, span_rows_)
+        base = jnp.where(row == s, spans[s], base)
         for w in range(WT):
-            n = span - (WT - 1) + w
-            j = slot_ref[jnp.maximum(n, 0)]
-            j = (j & ~15) | ((j & 3) << 2) | ((j >> 2) & 3)
-            seen[s * WT + w] = j
-            source[jnp.where(n >= 0, s * NSLOT + j, SLOTS * NSLOT)] = s * WT + w
-    lane = lax.broadcasted_iota(jnp.int32, (8, LANES), 1) % SPAN
-    qpos = span_rows_ * SPAN + lane
+            n = jnp.clip(spans[s] + (w - (WT - 1)), 0, NSLOT - 1)
+            seen[s * WT + w] = swap_fields(slot_ref[n])
+    qpos = base * SPAN + lax.broadcasted_iota(jnp.int32, (8, LANES), 1) % SPAN
     qstart = jnp.zeros((8, LANES), jnp.int32)
     end = 0
     for i in range(len_ref.shape[0]):
         end = end + len_ref[i]
         qstart = jnp.where(qpos >= end, end, qstart)
-    rows_ref[0] = qstart - (span_rows_ - (WT - 1)) * SPAN
-    rows_ref[1] = qpos - qstart
-
-
-def kernel(seen, source, rows_ref, q_ref, o_ref, k_ref, v_ref, dq_ref, dk_ref, dv_ref,
-           k_all, v_all, qm, om, qs, os_, ot, tq, s_scr, p_scr, wk, wv, inv_scr, dqm,
+    rows_scr[0] = qstart - (base - (WT - 1)) * SPAN
+    rows_scr[1] = qpos - qstart
+
+    def fill(i, _):
+        n = span_in(swap_fields(i))
+        for s in range(SLOTS):
+            t = jnp.minimum(jnp.maximum(n - spans[s] + WT, 0), WT + 1)
+            source[s * NSLOT + i] = s * PAD + t
+        return 0
+
+    lax.fori_loop(0, NSLOT, fill, 0, unroll=8)
+
+
+def kernel(slot_ref, len_ref, slot_row, q_ref, o_ref, k_ref, v_ref, dq_ref, dk_ref, dv_ref,
+           k_all, v_all, qm, om, qs, os_, ot, tq, s_scr, p_scr, wk, wv, inv_scr, dqm, seen, source, rows_ref,
            *rest):
     bufs_v, bufs_k = rest[:9], rest[9:18]
     send, recv, local = rest[18:]
@@ -449,6 +451,7 @@
         for copy in qo[i]:
             copy.start()
         own[2 + i].start()
+    make_tables(z * NY + y, slot_ref, slot_row, len_ref, seen, source, rows_ref)
     gk.near(1)
     gk.second()
     gk.finish(0)
@@ -490,8 +493,10 @@
         own[2 + i].wait()
 
     sub = lax.broadcasted_iota(jnp.int32, (SPAN, 1), 0)
-    wk[SLOTS * WT] = jnp.zeros((SPAN, HEAD), BF16)
-    wv[SLOTS * WT] = jnp.zeros((SPAN, HEAD), BF16)
+    for s in range(SLOTS):
+        for t in (0, WT + 1):
+            wk[s * PAD + t] = jnp.zeros((SPAN, HEAD), BF16)
+            wv[s * PAD + t] = jnp.zeros((SPAN, HEAD), BF16)
     mid = WT // 2
 
     def during(s, table):
@@ -504,7 +509,7 @@
 
     def dv_tile(s, t):
         dv = jnp.dot(p_scr[s, t], os_[s], preferred_element_type=F32)
-        wv[s * WT + t] = dv.astype(BF16)
+        wv[s * PAD + 1 + t] = dv.astype(BF16)
 
     def first_part(s, _):
         low, extra = rows_ref[0, pl.ds(s, 1), :], rows_ref[1, pl.ds(s, 1), :]
@@ -602,7 +607,7 @@
             ds = (p_scr[s, t].astype(F32) * (s_scr[t] - dots)).astype(BF16)
             p_scr[s, t] = ds
             dk = jnp.dot(ds, qs[s], preferred_element_type=F32) * SCALE
-            wk[s * WT + t] = dk.astype(BF16)
+            wk[s * PAD + 1 + t] = dk.astype(BF16)
         during(s, k_events[3])
         return 0
 
@@ -732,18 +737,6 @@
         vmem(2, NY, HALF, HEAD),
         vmem(FAR - 1, 2, NY, SPAN, HEAD),
     ]
-    seen, source, rows = pl.pallas_call(
-        tables_kernel,
-        out_shape=[
-            jax.ShapeDtypeStruct((SLOTS * WT,), jnp.int32),
-            jax.ShapeDtypeStruct((SLOTS * NSLOT + 8,), jnp.int32),
-            jax.ShapeDtypeStruct((2, 8, LANES), jnp.int32),
-        ],
-        in_specs=[smem] * 2,
-        out_specs=[smem, smem, pl.BlockSpec(memory_space=pltpu.VMEM)],
-        scratch_shapes=[pltpu.SMEM((NSLOT,), jnp.int32)],
-        name="tables",
-    )(span_slot, doc_lengths)
     outs = pl.pallas_call(
         kernel,
         out_shape=[
@@ -764,10 +757,13 @@
             vmem(HEAD, LANES),
             vmem(WT, SPAN, LANES, dtype=F32),
             vmem(SLOTS, WT, SPAN, LANES),
-            vmem(SLOTS * WT + 1, SPAN, HEAD),
-            vmem(SLOTS * WT + 1, SPAN, HEAD),
+            vmem(SLOTS * PAD, SPAN, HEAD),
+            vmem(SLOTS * PAD, SPAN, HEAD),
             vmem(SLOTS, 8, LANES, dtype=F32),
             vmem(SLOTS * SPAN, WIDE),
+            pltpu.SMEM((SLOTS * WT,), jnp.int32),
+            pltpu.SMEM((SLOTS * NSLOT,), jnp.int32),
+            vmem(2, 8, LANES, dtype=jnp.int32),
         ] + scatter_bufs * 2 + [
             pltpu.SemaphoreType.DMA((N_SEND,)),
             pltpu.SemaphoreType.DMA((N_RECV,)),
@@ -776,7 +772,7 @@
         compiler_params=pltpu.CompilerParams(
             collective_id=0, has_side_effects=True, vmem_limit_bytes=60 * 1024 * 1024),
         name="attention_backward",
-    )(seen, source, rows, queries, output_cotangent, keys, values)
+    )(span_slot, doc_lengths, span_slot.reshape(1, NSLOT), queries, output_cotangent, keys, values)
     outs = pl.pallas_call(
         settle_kernel,
         out_shape=[jax.ShapeDtypeStruct(out.shape, out.dtype) for out in outs],

time: 98.5 us -> 96.8 us (0.983)
  Pallas kernels: 97.5 us -> 96 us
    pallas_call x1 -> x0, Pallas kernels: 2.22 us -> none  [per_device(): pl.pallas_call(tables_kernel, out_shape=[jax.ShapeDtypeStruct((SLOTS * WT...]
where the time goes in v5:
time: 96.8 us; the launch traced here: 96.7 us
  Pallas kernels  96 us (99%)
    pallas_call x1, Pallas kernels, per_device(): pl.pallas_call(kernel, out_shape=[jax.ShapeDtypeStruct(queries.shape, BF1...  94.1 us

profile of v5, /device:TPU:2, one launch (start us, length us, event | category | flops | bytes accessed | tf_op | source)
XLA Modules:
  0.0 96.7 jit_solution(13564496927188702469)
XLA Ops:
  0.6 94.1 %attention_backward.1 = (bf16[64,4096]{1,0:T(8,128)(2,1)}, bf16[64,512]{1,0:T(8,128)(2,1)}, bf16[64,512]{1,0:T(8,128)(2,1)}) custom-call(s32[128]{0:T(128)} %slot_ref.1, s32[16]{0:T(128)} %len_ref.1, s32[1,128]{1,0:T(1,128)} %bitcast.1, bf16[64,4096]{1,0:T(8,128)(2,1)} %q_ref.1, bf16[64,4096]{1,0:T(8,128)(2,1)} %o_ref.1, bf16[64,512]{1,0:T(8,128)(2,1)} %k_ref.1, ...), custom_call_target="tpu_custom_call" | custom-call | tf_op jit(solution)/shard_map/attention_backward/pallas_call | solution.py:740
  94.7 1.9 %settle.1 = (bf16[64,4096]{1,0:T(8,128)(2,1)}, bf16[64,512]{1,0:T(8,128)(2,1)}, bf16[64,512]{1,0:T(8,128)(2,1)}) custom-call(bf16[64,4096]{1,0:T(8,128)(2,1)} %get-tuple-element.6.dq_in, bf16[64,512]{1,0:T(8,128)(2,1)} %get-tuple-element.7.dk_in, bf16[64,512]{1,0:T(8,128)(2,1)} %get-tuple-element.8.dv_in), custom_call_target="tpu_custom_call" | custom-call | tf_op jit(solution)/shard_map/settle/pallas_call | solution.py:776
